TPU v7x, 256 devices: a whole 4x4x8 slice. The times are simulated.
256 devices in a mesh: section: 4 (over y_hi, core), ctx: 8 (over y_lo, x), tp: 8 (over z).
Axes of the slice: x: 4, y: 4 (y_hi: 2, y_lo: 2; y = y_hi * 2 + y_lo), z: 8, core: 2. Of those that a mesh axis runs over, the one named last changes fastest.
Arguments:
- tokens: bfloat16 [2, 1024, 4096], P(None, 'ctx', 'tp'), may hold values from -60 to 60
- document_lengths: int32 [2], replicated, may hold values from 1 to 1024, 1536 in all
- tenant_indices: int32 [2], replicated, may hold values from 0 to 3
- attention_norm_gain: float32 [4, 4096], P('section'), may hold values from 0.5 to 1.5
- query_weight: bfloat16 [4, 4096, 4096], P('section', None, 'tp'), may hold values from -0.5625 to 0.5625
- key_weight: bfloat16 [4, 4096, 1024], P('section', None, 'tp'), may hold values from -0.5625 to 0.5625
- value_weight: bfloat16 [4, 4096, 1024], P('section', None, 'tp'), may hold values from -0.09375 to 0.09375
- output_weight: bfloat16 [4, 4096, 4096], P('section', 'tp'), may hold values from -0.09375 to 0.09375
- query_adapter_down: bfloat16 [4, 4, 4096, 16], P('section'), may hold values from -0.09375 to 0.09375
- query_adapter_up: bfloat16 [4, 4, 16, 4096], P('section', None, None, 'tp'), may hold values from -1.5 to 1.5
- value_adapter_down: bfloat16 [4, 4, 4096, 16], P('section'), may hold values from -0.09375 to 0.09375
- value_adapter_up: bfloat16 [4, 4, 16, 1024], P('section', None, None, 'tp'), may hold values from -1.5 to 1.5
- closing_norm_gain: float32 [4096], P('tp'), may hold values from 0.4 to 2.5
Outputs:
- embedding: float32 [2, 4096], P(None, 'tp')
Inputs may be any that keep to these rules, and one draw needn't show every extreme that they name: The first document_lengths[m] positions of document m are its tokens.
All inputs are finite; a program needn't handle non-finite values.
Results may differ from a plain program's by a relative error of at most 0.03.
Values may be sent and summed in bfloat16 or wider, within the bound.
A program may use at most 128 MiB of HBM per device.

v0:
```python
import jax
import jax.numpy as jnp
from jax import lax
from jax.sharding import PartitionSpec as P

HEAD_SIZE = 128


def shifted(array, axis, by):
    length = lax.axis_size(axis)
    pairs = [(i, i + by) for i in range(length) if 0 <= i + by < length]
    return lax.ppermute(array, axis, pairs)


def rms_scale(values, gain, epsilon):
    return values * lax.rsqrt(jnp.mean(values * values, axis=-1, keepdims=True) + epsilon) * gain


def rotate(values, token_positions):
    half = values.shape[-1] // 2
    freq = 500000.0 ** (-jnp.arange(half, dtype=jnp.float32) / half)
    angle = token_positions[:, None] * freq[None, :]
    cosine = jnp.cos(angle)[:, None, :]
    sine = jnp.sin(angle)[:, None, :]
    first = values[..., :half]
    second = values[..., half:]
    return jnp.concatenate(
        [first * cosine - second * sine, second * cosine + first * sine], axis=-1
    )


def shards(
    tokens,
    document_lengths,
    tenant_indices,
    attention_norm_gain,
    query_weight,
    key_weight,
    value_weight,
    output_weight,
    query_adapter_down,
    query_adapter_up,
    value_adapter_down,
    value_adapter_up,
    closing_norm_gain,
):
    micro, rows, width = tokens.shape
    sections = lax.axis_size("section")
    section = lax.axis_index("section")
    full_width = width * lax.axis_size("tp")
    query_width = query_weight.shape[2]
    kv_width = key_weight.shape[2]
    local_heads = query_width // HEAD_SIZE
    local_kv = kv_width // HEAD_SIZE
    group = local_heads // local_kv
    slots = lax.axis_index("ctx") * rows + jnp.arange(rows, dtype=jnp.int32)
    token_positions = slots.astype(jnp.float32)
    out_rows = output_weight[0]
    incoming = jnp.zeros((rows, width), jnp.bfloat16)
    finals = []
    for tick in range(micro + sections - 1):
        inbound = tokens[tick] if tick < micro else jnp.zeros((rows, width), jnp.bfloat16)
        current = jnp.where(section == 0, inbound, incoming)
        index = jnp.clip(tick - section, 0, micro - 1)
        document_length = document_lengths[index]
        tenant_adapter = tenant_indices[index]
        whole = lax.all_gather(current, "tp", axis=1, tiled=True)
        widen = current.astype(jnp.float32)
        normalized_state = rms_scale(
            whole.astype(jnp.float32), attention_norm_gain[0], 1e-05
        ).astype(jnp.bfloat16)
        query_down_map = lax.dynamic_index_in_dim(
            query_adapter_down[0], tenant_adapter, 0, keepdims=False
        )
        query_up_map = lax.dynamic_index_in_dim(
            query_adapter_up[0], tenant_adapter, 0, keepdims=False
        )
        value_down_map = lax.dynamic_index_in_dim(
            value_adapter_down[0], tenant_adapter, 0, keepdims=False
        )
        value_up_map = lax.dynamic_index_in_dim(
            value_adapter_up[0], tenant_adapter, 0, keepdims=False
        )
        query_low_rank = jnp.dot(
            normalized_state, query_down_map, preferred_element_type=jnp.float32
        ).astype(jnp.bfloat16)
        value_low_rank = jnp.dot(
            normalized_state, value_down_map, preferred_element_type=jnp.float32
        ).astype(jnp.bfloat16)
        query_rows = jnp.dot(
            normalized_state, query_weight[0], preferred_element_type=jnp.float32
        ) + jnp.dot(query_low_rank, query_up_map, preferred_element_type=jnp.float32)
        query_rows = rotate(
            query_rows.reshape(rows, local_heads, HEAD_SIZE), token_positions
        ).astype(jnp.bfloat16)
        key = rotate(
            jnp.dot(normalized_state, key_weight[0], preferred_element_type=jnp.float32).reshape(
                rows, local_kv, HEAD_SIZE
            ),
            token_positions,
        )
        key = key.astype(jnp.bfloat16).reshape(rows, kv_width)
        value_rows = jnp.dot(
            normalized_state, value_weight[0], preferred_element_type=jnp.float32
        ) + jnp.dot(value_low_rank, value_up_map, preferred_element_type=jnp.float32)
        value_rows = value_rows.astype(jnp.bfloat16)
        keys = lax.all_gather(key, "ctx", axis=0, tiled=True)
        values = lax.all_gather(value_rows, "ctx", axis=0, tiled=True)
        total = keys.shape[0]
        keys = keys.reshape(total, local_kv, HEAD_SIZE)
        values = values.reshape(total, local_kv, HEAD_SIZE)
        grouped = query_rows.reshape(rows, local_kv, group, HEAD_SIZE)
        scores = jnp.einsum(
            "rkgd,skd->kgrs", grouped, keys, preferred_element_type=jnp.float32
        ) * HEAD_SIZE ** (-0.5)
        attend_valid = jnp.arange(total, dtype=jnp.int32) < document_length
        scores = jnp.where(attend_valid, scores, -1e30)
        top = jnp.max(scores, axis=-1, keepdims=True)
        expo = jnp.exp(scores - top)
        weights = (expo / jnp.sum(expo, axis=-1, keepdims=True)).astype(jnp.bfloat16)
        mixed = jnp.einsum("kgrs,skd->rkgd", weights, values, preferred_element_type=jnp.float32)
        mixed = mixed.astype(jnp.bfloat16).reshape(rows, query_width)
        update = lax.psum_scatter(
            jnp.dot(mixed, out_rows, preferred_element_type=jnp.float32).astype(jnp.bfloat16),
            "tp",
            scatter_dimension=1,
            tiled=True,
        ).astype(jnp.float32)
        hidden_state = (widen + update).astype(jnp.bfloat16)
        if tick >= sections - 1:
            finals.append(hidden_state)
        if tick < micro + sections - 2:
            incoming = shifted(hidden_state, "section", 1)
    stacked = jnp.stack(finals).astype(jnp.float32)
    squares = lax.psum(jnp.sum(stacked * stacked, axis=-1), "tp")
    scaled = stacked * lax.rsqrt(squares[..., None] / full_width + 1e-05) * closing_norm_gain
    valid = slots[None, :] < document_lengths[:, None]
    partial_value = jnp.sum(jnp.where(valid[..., None], scaled, 0.0), axis=1) / document_lengths[
        :, None
    ].astype(jnp.float32)
    pooled = lax.psum(jnp.where(section == sections - 1, partial_value, 0.0), ("section", "ctx"))
    norms = lax.psum(jnp.sum(pooled * pooled, axis=-1), "tp")
    return pooled * lax.rsqrt(norms[:, None] / full_width + 1e-06)


def solution(mesh):
    placed = (
        P(None, "ctx", "tp"),
        P(),
        P(),
        P("section", None),
        P("section", None, "tp"),
        P("section", None, "tp"),
        P("section", None, "tp"),
        P("section", "tp", None),
        P("section", None, None, None),
        P("section", None, None, "tp"),
        P("section", None, None, None),
        P("section", None, None, "tp"),
        P("tp"),
    )
    return jax.shard_map(
        shards, mesh=mesh, in_specs=placed, out_specs=P(None, "tp"), check_vma=False
    )
```

profile of v0, /device:TPU:1, one launch (start us, length us, event | category | flops | bytes accessed | tf_op | source)
XLA Modules:
  0.0 845.0 jit_solution(16937888072392111333)
XLA Ops:
  6.5 1.7 slice_select_fusion
  8.3 1.6 fusion.303
  12.9 33.7 %all-gather.15.cloned.1.call-done = bf16[1,128,4096]{2,1,0:T(8,128)(2,1)} async-done(((bf16[1,128,512]{2,1,0:T(8,128)(2,1)}), bf16[1,128,4096]{2,1,0:T(8,128)(2,1)}) %all-gather.15.cloned.1.call-update) | async-done | bytes 1048592 | tf_op jit(solution)/shard_map/all_gather | solution.py:67
  46.6 1.6 fusion.27
  48.2 1.8 convolution_bitcast_fusion.4
  50.3 1.8 fusion.79
  53.7 20.3 %all_gather.46 = bf16[1024,128]{0,1:T(8,128)(2,1)S(1)} all-gather(bf16[128,128]{0,1:T(8,128)(2,1)S(1)} %fusion.52), channel_id=1, replica_groups=mesh['section'=4,'ctx'=8,'tp'=8] {'ctx'}, dimensions={0}, use_global_device_ids=true | all-gather | bytes 294912 | tf_op jit(solution)/shard_map/all_gather | solution.py:108
  74.0 19.7 %all_gather.47 = bf16[1024,128]{0,1:T(8,128)(2,1)S(1)} all-gather(bf16[128,128]{0,1:T(8,128)(2,1)S(1)} %pad_maximum_fusion.1), channel_id=1, replica_groups=mesh['section'=4,'ctx'=8,'tp'=8] {'ctx'}, dimensions={0}, use_global_device_ids=true | all-gather | bytes 294912 | tf_op jit(solution)/shard_map/all_gather | solution.py:107
  93.7 3.7 fusion.13
  97.4 1.7 convolution_add_fusion
  102.7 1.7 convolution_convert_fusion.4
  104.5 44.7 %reduce-scatter.6.cloned.1.call-done = bf16[128,512]{1,0:T(8,128)(2,1)} async-done(((bf16[128,4096]{1,0:T(8,128)(2,1)}), bf16[128,512]{1,0:T(8,128)(2,1)}) %reduce-scatter.6.cloned.1.call-update) | async-done | bytes 131088 | tf_op jit(solution)/shard_map/reduce_scatter | solution.py:123
  150.2 10.1 %collective-permute-start = (bf16[128,512]{1,0:T(8,128)(2,1)S(1)}, bf16[128,512]{1,0:T(8,128)(2,1)S(1)}, u32[]{:S(2)}, u32[]{:S(2)}) collective-permute-start(bf16[128,512]{1,0:T(8,128)(2,1)S(1)} %fusion.85), channel_id=1, source_target_pairs={{0,64},{64,128},{128,192},{1,65},{65,129},{129,193},{2,66},{66,130... | collective-permute-start | bytes 393224 | tf_op jit(solution)/shard_map/ppermute | solution.py:12
  160.3 1.9 collective-permute-done
  165.5 30.6 %all-gather.7.cloned.1.call-done = bf16[128,4096]{1,0:T(8,128)(2,1)} async-done(((bf16[128,512]{1,0:T(8,128)(2,1)}), bf16[128,4096]{1,0:T(8,128)(2,1)}) %all-gather.7.cloned.1.call-update) | async-done | bytes 1048592 | tf_op jit(solution)/shard_map/all_gather | solution.py:67
  196.1 1.6 fusion.15
  197.7 1.8 convolution_bitcast_fusion.3
  199.8 20.3 %all_gather.50 = bf16[1024,128]{0,1:T(8,128)(2,1)S(1)} all-gather(bf16[128,128]{0,1:T(8,128)(2,1)S(1)} %pad_maximum_fusion.2), channel_id=1, replica_groups=mesh['section'=4,'ctx'=8,'tp'=8] {'ctx'}, dimensions={0}, use_global_device_ids=true | all-gather | bytes 294912 | tf_op jit(solution)/shard_map/all_gather | solution.py:107
  221.6 1.9 fusion.53
  223.5 19.8 %all_gather.49 = bf16[1024,128]{0,1:T(8,128)(2,1)S(1)} all-gather(bf16[128,128]{0,1:T(8,128)(2,1)S(1)} %fusion.53), channel_id=1, replica_groups=mesh['section'=4,'ctx'=8,'tp'=8] {'ctx'}, dimensions={0}, use_global_device_ids=true | all-gather | bytes 294912 | tf_op jit(solution)/shard_map/all_gather | solution.py:108
  243.3 1.6 fusion.61
  244.9 3.0 fusion.40
  251.7 1.7 convolution_convert_fusion.3
  253.4 45.2 %reduce-scatter.8.cloned.1.call-done = bf16[128,512]{1,0:T(8,128)(2,1)} async-done(((bf16[128,4096]{1,0:T(8,128)(2,1)}), bf16[128,512]{1,0:T(8,128)(2,1)}) %reduce-scatter.8.cloned.1.call-update) | async-done | bytes 131088 | tf_op jit(solution)/shard_map/reduce_scatter | solution.py:123
  299.6 9.7 %collective-permute-start.1 = (bf16[128,512]{1,0:T(8,128)(2,1)S(1)}, bf16[128,512]{1,0:T(8,128)(2,1)S(1)}, u32[]{:S(2)}, u32[]{:S(2)}) collective-permute-start(bf16[128,512]{1,0:T(8,128)(2,1)S(1)} %add_convert_fusion.6), channel_id=1, source_target_pairs={{0,64},{64,128},{128,192},{1,65},{65,129},{129,193},{2,66},{66,130... | collective-permute-start | bytes 393224 | tf_op jit(solution)/shard_map/ppermute | solution.py:12
  309.3 1.9 collective-permute-done.1
  314.5 30.6 %all-gather.9.cloned.1.call-done = bf16[128,4096]{1,0:T(8,128)(2,1)} async-done(((bf16[128,512]{1,0:T(8,128)(2,1)}), bf16[128,4096]{1,0:T(8,128)(2,1)}) %all-gather.9.cloned.1.call-update) | async-done | bytes 1048592 | tf_op jit(solution)/shard_map/all_gather | solution.py:67
  345.1 1.6 fusion.18
  346.7 1.8 convolution_bitcast_fusion.2
  348.8 20.3 %all_gather.53 = bf16[1024,128]{0,1:T(8,128)(2,1)S(1)} all-gather(bf16[128,128]{0,1:T(8,128)(2,1)S(1)} %pad_maximum_fusion.3), channel_id=1, replica_groups=mesh['section'=4,'ctx'=8,'tp'=8] {'ctx'}, dimensions={0}, use_global_device_ids=true | all-gather | bytes 294912 | tf_op jit(solution)/shard_map/all_gather | solution.py:107
  370.6 1.9 fusion.54
  372.5 19.6 %all_gather.52 = bf16[1024,128]{0,1:T(8,128)(2,1)S(1)} all-gather(bf16[128,128]{0,1:T(8,128)(2,1)S(1)} %fusion.54), channel_id=1, replica_groups=mesh['section'=4,'ctx'=8,'tp'=8] {'ctx'}, dimensions={0}, use_global_device_ids=true | all-gather | bytes 294912 | tf_op jit(solution)/shard_map/all_gather | solution.py:108
  392.1 1.6 fusion.62
  393.7 2.9 fusion.43
  398.3 1.5 convolution_convert_fusion.7
  400.5 1.7 convolution_convert_fusion.2
  402.3 45.1 %reduce-scatter.10.cloned.1.call-done = bf16[128,512]{1,0:T(8,128)(2,1)} async-done(((bf16[128,4096]{1,0:T(8,128)(2,1)}), bf16[128,512]{1,0:T(8,128)(2,1)}) %reduce-scatter.10.cloned.1.call-update) | async-done | bytes 131088 | tf_op jit(solution)/shard_map/reduce_scatter | solution.py:123
  448.3 9.7 %collective-permute-start.2 = (bf16[128,512]{1,0:T(8,128)(2,1)S(1)}, bf16[128,512]{1,0:T(8,128)(2,1)S(1)}, u32[]{:S(2)}, u32[]{:S(2)}) collective-permute-start(bf16[128,512]{1,0:T(8,128)(2,1)S(1)} %add_convert_fusion.4), channel_id=1, source_target_pairs={{0,64},{64,128},{128,192},{1,65},{65,129},{129,193},{2,66},{66,130... | collective-permute-start | bytes 393224 | tf_op jit(solution)/shard_map/ppermute | solution.py:12
  458.0 1.9 collective-permute-done.2
  463.1 30.6 %all-gather.11.cloned.1.call-done = bf16[128,4096]{1,0:T(8,128)(2,1)} async-done(((bf16[128,512]{1,0:T(8,128)(2,1)}), bf16[128,4096]{1,0:T(8,128)(2,1)}) %all-gather.11.cloned.1.call-update) | async-done | bytes 1048592 | tf_op jit(solution)/shard_map/all_gather | solution.py:67
  493.8 1.6 fusion.21
  495.4 1.8 convolution_bitcast_fusion.1
  497.5 20.5 %all_gather.56 = bf16[1024,128]{0,1:T(8,128)(2,1)S(1)} all-gather(bf16[128,128]{0,1:T(8,128)(2,1)S(1)} %pad_maximum_fusion.4), channel_id=1, replica_groups=mesh['section'=4,'ctx'=8,'tp'=8] {'ctx'}, dimensions={0}, use_global_device_ids=true | all-gather | bytes 294912 | tf_op jit(solution)/shard_map/all_gather | solution.py:107
  519.6 1.9 fusion.55
  521.4 19.6 %all_gather.55 = bf16[1024,128]{0,1:T(8,128)(2,1)S(1)} all-gather(bf16[128,128]{0,1:T(8,128)(2,1)S(1)} %fusion.55), channel_id=1, replica_groups=mesh['section'=4,'ctx'=8,'tp'=8] {'ctx'}, dimensions={0}, use_global_device_ids=true | all-gather | bytes 294912 | tf_op jit(solution)/shard_map/all_gather | solution.py:108
  541.1 1.6 fusion.63
  542.7 2.9 fusion.46
  549.4 1.7 convolution_convert_fusion.1
  551.2 44.6 %reduce-scatter.12.cloned.1.call-done = bf16[128,512]{1,0:T(8,128)(2,1)} async-done(((bf16[128,4096]{1,0:T(8,128)(2,1)}), bf16[128,512]{1,0:T(8,128)(2,1)}) %reduce-scatter.12.cloned.1.call-update) | async-done | bytes 131088 | tf_op jit(solution)/shard_map/reduce_scatter | solution.py:123
  596.8 10.1 %collective-permute-start.3 = (bf16[128,512]{1,0:T(8,128)(2,1)S(1)}, bf16[128,512]{1,0:T(8,128)(2,1)S(1)}, u32[]{:S(2)}, u32[]{:S(2)}) collective-permute-start(bf16[128,512]{1,0:T(8,128)(2,1)S(1)} %add_convert_fusion.2), channel_id=1, source_target_pairs={{0,64},{64,128},{128,192},{1,65},{65,129},{129,193},{2,66},{66,130... | collective-permute-start | bytes 393224 | tf_op jit(solution)/shard_map/ppermute | solution.py:12
  606.9 1.9 collective-permute-done.3
  612.6 30.1 %all-gather.13.cloned.1.call-done = bf16[128,4096]{1,0:T(8,128)(2,1)} async-done(((bf16[128,512]{1,0:T(8,128)(2,1)}), bf16[128,4096]{1,0:T(8,128)(2,1)}) %all-gather.13.cloned.1.call-update) | async-done | bytes 1048592 | tf_op jit(solution)/shard_map/all_gather | solution.py:67
  642.7 1.6 fusion.24
  644.4 1.8 convolution_bitcast_fusion
  646.5 20.3 %all_gather.59 = bf16[1024,128]{0,1:T(8,128)(2,1)S(1)} all-gather(bf16[128,128]{0,1:T(8,128)(2,1)S(1)} %pad_maximum_fusion.5), channel_id=1, replica_groups=mesh['section'=4,'ctx'=8,'tp'=8] {'ctx'}, dimensions={0}, use_global_device_ids=true | all-gather | bytes 294912 | tf_op jit(solution)/shard_map/all_gather | solution.py:107
  668.3 1.9 fusion.56
  670.2 19.6 %all_gather.58 = bf16[1024,128]{0,1:T(8,128)(2,1)S(1)} all-gather(bf16[128,128]{0,1:T(8,128)(2,1)S(1)} %fusion.56), channel_id=1, replica_groups=mesh['section'=4,'ctx'=8,'tp'=8] {'ctx'}, dimensions={0}, use_global_device_ids=true | all-gather | bytes 294912 | tf_op jit(solution)/shard_map/all_gather | solution.py:108
  689.8 1.6 fusion.64
  691.4 2.9 fusion.49
  698.3 1.7 convolution_convert_fusion
  700.1 44.6 %reduce-scatter.14.cloned.1.call-done = bf16[128,512]{1,0:T(8,128)(2,1)} async-done(((bf16[128,4096]{1,0:T(8,128)(2,1)}), bf16[128,512]{1,0:T(8,128)(2,1)}) %reduce-scatter.14.cloned.1.call-update) | async-done | bytes 131088 | tf_op jit(solution)/shard_map/reduce_scatter | solution.py:123
  745.8 12.1 %psum.21 = f32[2,128]{1,0:T(2,128)S(1)} all-reduce(f32[2,128]{1,0:T(2,128)S(1)} %fusion.81), channel_id=1, replica_groups=mesh['section'=4,'ctx'=8,'tp'=8] {'tp'}, use_global_device_ids=true, to_apply=%region_21.22 | all-reduce | flops 256 | bytes 2048 | tf_op jit(solution)/shard_map/psum | solution.py:135
  758.2 68.1 %psum.22 = f32[2,512]{1,0:T(2,128)S(1)} all-reduce(f32[2,512]{1,0:T(2,128)S(1)} %divide_select_fusion), channel_id=1, replica_groups=mesh['section'=4,'ctx'=8,'tp'=8] {'section','ctx'}, use_global_device_ids=true, to_apply=%region_23.24 | all-reduce | flops 1024 | bytes 8192 | tf_op jit(solution)/shard_map/psum | solution.py:141
  826.5 11.0 %psum.23 = f32[2]{0:T(128)S(1)} all-reduce(f32[2]{0:T(128)S(1)} %multiply_reduce_fusion), channel_id=1, replica_groups=mesh['section'=4,'ctx'=8,'tp'=8] {'tp'}, use_global_device_ids=true, to_apply=%region_25.26 | all-reduce | flops 2 | bytes 16 | tf_op jit(solution)/shard_map/psum | solution.py:142
  (160 shorter events, 39.3 us)
Async XLA Ops:
  6.5 41.7 %copy-start = (bf16[1,4096,128]{2,1,0:T(8,128)(2,1)S(1)}, bf16[1,4096,128]{2,1,0:T(8,128)(2,1)}, u32[]{:S(2)}) copy-start(bf16[1,4096,128]{2,1,0:T(8,128)(2,1)} %param.18) | copy-start | bytes 3145732
  6.5 40.0 %all-gather.15.cloned.1.call-start = ((), (), s32[]{:S(2)}) async-start(), calls=%async_computation.14 | async-start | bytes 1179648 | tf_op jit(solution)/shard_map/all_gather | solution.py:67
  6.5 43.7 %copy-start.13 = (f32[1,4096]{1,0:T(1,128)S(1)}, f32[1,4096]{1,0:T(1,128)}, u32[]{:S(2)}) copy-start(f32[1,4096]{1,0:T(1,128)} %param.16) | copy-start | bytes 49156
  8.2 141.0 %reduce-scatter.6.cloned.1.call-start = ((), (), s32[]{:S(2)}) async-start(), calls=%async_computation.5 | async-start | bytes 1179648 | tf_op jit(solution)/shard_map/reduce_scatter | solution.py:123
  11.9 336.6 %copy-start.14 = (f32[64]{0:T(128)}, f32[64]{0:T(128)S(1)}, u32[]{:S(2)}) copy-start(f32[64]{0:T(128)S(1)} %multiply_power_fusion) | copy-start | bytes 772
  12.0 336.6 %copy-start.17 = (f32[128]{0:T(128)}, f32[128]{0:T(128)S(1)}, u32[]{:S(2)}) copy-start(f32[128]{0:T(128)S(1)} %fusion.262) | copy-start | bytes 1540
  46.6 3.7 copy-start.11
  48.2 3.9 copy-start.27
  93.7 3.7 copy-start.26
  100.5 2.2 copy-start.1
  102.7 46.5 %copy-start.12 = (bf16[2,128,512]{2,1,0:T(8,128)(2,1)S(1)}, bf16[2,128,512]{2,1,0:T(8,128)(2,1)}, u32[]{:S(2)}) copy-start(bf16[2,128,512]{2,1,0:T(8,128)(2,1)} %param.13) | copy-start | bytes 786436
  104.5 91.6 %all-gather.7.cloned.1.call-start = ((), (), s32[]{:S(2)}) async-start(), calls=%async_computation.6 | async-start | bytes 1179648 | tf_op jit(solution)/shard_map/all_gather | solution.py:67
  150.2 12.0 %collective-permute-start = (bf16[128,512]{1,0:T(8,128)(2,1)S(1)}, bf16[128,512]{1,0:T(8,128)(2,1)S(1)}, u32[]{:S(2)}, u32[]{:S(2)}) collective-permute-start(bf16[128,512]{1,0:T(8,128)(2,1)S(1)} %fusion.85), channel_id=1, source_target_pairs={{0,64},{64,128},{128,192},{1,65},{65,129},{129,193},{2,66},{66,130... | collective-permute-start | bytes 393224 | tf_op jit(solution)/shard_map/ppermute | solution.py:12
  162.9 135.8 %reduce-scatter.8.cloned.1.call-start = ((), (), s32[]{:S(2)}) async-start(), calls=%async_computation.7 | async-start | bytes 1179648 | tf_op jit(solution)/shard_map/reduce_scatter | solution.py:123
  196.1 24.0 %copy-start.9 = (bf16[128,4096]{1,0:T(8,128)(2,1)S(1)}, bf16[128,4096]{1,0:T(8,128)(2,1)}, u32[]{:S(2)}) copy-start(bf16[128,4096]{1,0:T(8,128)(2,1)} %all-gather.7.cloned.1.call-done) | copy-start | bytes 3145732
  249.5 2.2 copy-start.2
  251.6 47.0 %copy-start.10 = (bf16[128,512]{1,0:T(8,128)(2,1)S(1)}, bf16[128,512]{1,0:T(8,128)(2,1)}, u32[]{:S(2)}) copy-start(bf16[128,512]{1,0:T(8,128)(2,1)} %bitcast_select_fusion.5) | copy-start | bytes 393220
  253.4 91.7 %all-gather.9.cloned.1.call-start = ((), (), s32[]{:S(2)}) async-start(), calls=%async_computation.8 | async-start | bytes 1179648 | tf_op jit(solution)/shard_map/all_gather | solution.py:67
  299.6 11.6 %collective-permute-start.1 = (bf16[128,512]{1,0:T(8,128)(2,1)S(1)}, bf16[128,512]{1,0:T(8,128)(2,1)S(1)}, u32[]{:S(2)}, u32[]{:S(2)}) collective-permute-start(bf16[128,512]{1,0:T(8,128)(2,1)S(1)} %add_convert_fusion.6), channel_id=1, source_target_pairs={{0,64},{64,128},{128,192},{1,65},{65,129},{129,193},{2,66},{66,130... | collective-permute-start | bytes 393224 | tf_op jit(solution)/shard_map/ppermute | solution.py:12
  311.9 135.5 %reduce-scatter.10.cloned.1.call-start = ((), (), s32[]{:S(2)}) async-start(), calls=%async_computation.9 | async-start | bytes 1179648 | tf_op jit(solution)/shard_map/reduce_scatter | solution.py:123
  314.5 83.3 %copy-start.22 = (pred[1024]{0:T(1024)(128)(4,1)}, pred[1024]{0:T(1024)(128)(4,1)S(1)}, u32[]{:S(2)}) copy-start(pred[1024]{0:T(1024)(128)(4,1)S(1)} %iota_compare_fusion.2) | copy-start | bytes 3076
  345.1 24.0 %copy-start.7 = (bf16[128,4096]{1,0:T(8,128)(2,1)S(1)}, bf16[128,4096]{1,0:T(8,128)(2,1)}, u32[]{:S(2)}) copy-start(bf16[128,4096]{1,0:T(8,128)(2,1)} %all-gather.9.cloned.1.call-done) | copy-start | bytes 3145732
  398.3 2.2 copy-start.3
  402.2 95.0 %copy-start.15 = (f32[64]{0:T(128)S(1)}, f32[64]{0:T(128)}, u32[]{:S(2)}) copy-start(f32[64]{0:T(128)} %copy-done.14) | copy-start | bytes 772
  402.2 95.0 %copy-start.18 = (f32[128]{0:T(128)S(1)}, f32[128]{0:T(128)}, u32[]{:S(2)}) copy-start(f32[128]{0:T(128)} %copy-done.17) | copy-start | bytes 1540
  402.2 91.5 %all-gather.11.cloned.1.call-start = ((), (), s32[]{:S(2)}) async-start(), calls=%async_computation.10 | async-start | bytes 1179648 | tf_op jit(solution)/shard_map/all_gather | solution.py:67
  448.3 11.6 %collective-permute-start.2 = (bf16[128,512]{1,0:T(8,128)(2,1)S(1)}, bf16[128,512]{1,0:T(8,128)(2,1)S(1)}, u32[]{:S(2)}, u32[]{:S(2)}) collective-permute-start(bf16[128,512]{1,0:T(8,128)(2,1)S(1)} %add_convert_fusion.4), channel_id=1, source_target_pairs={{0,64},{64,128},{128,192},{1,65},{65,129},{129,193},{2,66},{66,130... | collective-permute-start | bytes 393224 | tf_op jit(solution)/shard_map/ppermute | solution.py:12
  460.6 135.3 %reduce-scatter.12.cloned.1.call-start = ((), (), s32[]{:S(2)}) async-start(), calls=%async_computation.11 | async-start | bytes 1179648 | tf_op jit(solution)/shard_map/reduce_scatter | solution.py:123
  463.1 83.6 %copy-start.23 = (pred[1024]{0:T(1024)(128)(4,1)}, pred[1024]{0:T(1024)(128)(4,1)S(1)}, u32[]{:S(2)}) copy-start(pred[1024]{0:T(1024)(128)(4,1)S(1)} %iota_compare_fusion.1) | copy-start | bytes 3076
  493.8 24.2 %copy-start.8 = (bf16[128,4096]{1,0:T(8,128)(2,1)S(1)}, bf16[128,4096]{1,0:T(8,128)(2,1)}, u32[]{:S(2)}) copy-start(bf16[128,4096]{1,0:T(8,128)(2,1)} %all-gather.11.cloned.1.call-done) | copy-start | bytes 3145732
  547.2 2.2 copy-start.4
  551.2 95.0 %copy-start.16 = (f32[64]{0:T(128)S(1)}, f32[64]{0:T(128)}, u32[]{:S(2)}) copy-start(f32[64]{0:T(128)} %copy-done.14) | copy-start | bytes 772
  551.2 95.0 %copy-start.19 = (f32[128]{0:T(128)S(1)}, f32[128]{0:T(128)}, u32[]{:S(2)}) copy-start(f32[128]{0:T(128)} %copy-done.17) | copy-start | bytes 1540
  551.2 91.5 %all-gather.13.cloned.1.call-start = ((), (), s32[]{:S(2)}) async-start(), calls=%async_computation.12 | async-start | bytes 1179648 | tf_op jit(solution)/shard_map/all_gather | solution.py:67
  596.8 12.0 %collective-permute-start.3 = (bf16[128,512]{1,0:T(8,128)(2,1)S(1)}, bf16[128,512]{1,0:T(8,128)(2,1)S(1)}, u32[]{:S(2)}, u32[]{:S(2)}) collective-permute-start(bf16[128,512]{1,0:T(8,128)(2,1)S(1)} %add_convert_fusion.2), channel_id=1, source_target_pairs={{0,64},{64,128},{128,192},{1,65},{65,129},{129,193},{2,66},{66,130... | collective-permute-start | bytes 393224 | tf_op jit(solution)/shard_map/ppermute | solution.py:12
  609.5 135.2 %reduce-scatter.14.cloned.1.call-start = ((), (), s32[]{:S(2)}) async-start(), calls=%async_computation.13 | async-start | bytes 1179648 | tf_op jit(solution)/shard_map/reduce_scatter | solution.py:123
  642.7 24.0 %copy-start.6 = (bf16[128,4096]{1,0:T(8,128)(2,1)S(1)}, bf16[128,4096]{1,0:T(8,128)(2,1)}, u32[]{:S(2)}) copy-start(bf16[128,4096]{1,0:T(8,128)(2,1)} %all-gather.13.cloned.1.call-done) | copy-start | bytes 3145732
  644.4 45.4 %copy-start.25 = (f32[128]{0:T(128)}, f32[128]{0:T(128)S(1)}, u32[]{:S(2)}) copy-start(f32[128]{0:T(128)S(1)} %add_rsqrt_fusion.2) | copy-start | bytes 1540
  694.3 0.7 copy-start.21
  696.1 2.2 copy-start.5
  698.3 1.8 copy-start.20
  698.3 59.7 %copy-start.24 = (f32[512]{0:T(512)S(1)}, f32[512]{0:T(512)}, u32[]{:S(2)}) copy-start(f32[512]{0:T(512)} %param.25) | copy-start | bytes 6148
Sparse Core Ops, SparseCore 0:
  9.2 37.3 all-gather.14
  104.6 44.5 reduce-scatter.5
  163.0 33.0 all-gather.6
  253.5 45.0 reduce-scatter.7
  312.0 33.0 all-gather.8
  402.3 44.9 reduce-scatter.9
  460.7 33.0 all-gather.10
  551.3 44.5 reduce-scatter.11
  609.7 33.0 all-gather.12
  700.2 44.5 reduce-scatter.13
where the time goes:
time: 853 us; the launch traced here: 845 us
  waiting for transfers between devices  388 us (45%)
  blocking collectives  291 us (34%)
  matrix products  66.3 us (8%)
  starting transfers between devices  39.9 us (5%)
  other arithmetic  26.5 us (3%)
  between operations  24 us (3%)
  local copies, waits for them, and re-layouts  9.4 us (1%)
    reduce_scatter x5, waiting for transfers between devices, shards(): lax.psum_scatter(jnp.dot(mixed, out_rows, preferred_element_type=jnp.floa...  224 us
    all_gather x5, waiting for transfers between devices, shards(): whole = lax.all_gather(current, 'tp', axis=1, tiled=True)  156 us
    all_gather x5, blocking collectives, shards(): keys = lax.all_gather(key, 'ctx', axis=0, tiled=True)  101 us
    all_gather x5, blocking collectives, shards(): values = lax.all_gather(value_rows, 'ctx', axis=0, tiled=True)  99 us
    psum x1, blocking collectives, shards(): lax.psum(jnp.where(section == sections - 1, partial_value, 0.0), ('sectio...  68.1 us
    ppermute x4, starting transfers between devices, shifted(): return lax.ppermute(array, axis, pairs)  39.5 us
  transfers between devices with their start and end apart: 14, of which 14 were waited for; matrix products, arithmetic and copies ran while one was open for 1% of the time, Pallas kernels for 0%

commit v1 on v0

v1 whole, which is shorter than its diff:
```python
import math

import jax
import jax.numpy as jnp
import numpy as np
from jax import lax
from jax.experimental import pallas as pl
from jax.experimental.pallas import tpu as pltpu
from jax.sharding import PartitionSpec as P

HEAD = 128
F32 = jnp.float32
BF16 = jnp.bfloat16
MESH = pl.DeviceIdType.MESH

PIECES = 2
FAR = 3
WK, WV, WQ, GAIN, WO, DOWN, UP = range(7)
NEAR = ((1, 0), (0, 1), (0, 3))
REST = ((1, 1), (1, 3), (0, 2), (1, 2))


def fold(x):
    total = x[:, :HEAD]
    for i in range(1, x.shape[1] // HEAD):
        total = total + x[:, i * HEAD:(i + 1) * HEAD]
    return total


def kernel(
    sizes,
    lengths, tenants, tokens, gain_hbm, closing, tables, wq_hbm, wk_hbm, wv_hbm, wo_hbm,
    qd_hbm, vd_hbm, q_up, v_up,
    out,
    wq, wkv, wo, gains, qd, vd, down, up, trig,
    hidden, own, agb, agf, rsb, rsf, rso, rsfo, prt, kvbuf,
    acc_q, acc_kv, acc_l, squares, qbuf, att, terms,
    ssb, ppb, sqb, res,
    w_sem, w_send, small_sem, in_sem, ag_send, ag_recv, rs_send, rs_recv, prt_recv,
    kv_send, kv_recv, pass_send, pass_recv, ss_send, ss_recv, pp_send, pp_recv, sq_send, sq_recv,
    fin_send, fin_recv,
):
    sections, n_ctx, n_tp, micro, rows, width = sizes
    full_width = width * n_tp
    part = rows // PIECES
    heads = wq.shape[3] // HEAD
    rank = q_up.shape[1]
    s = lax.axis_index("section")
    c = lax.axis_index("ctx")
    z = lax.axis_index("tp")
    e = lax.rem(s, 2)
    first_pair = s < 2
    last_pair = s >= sections - 2
    partner = s + 1 - 2 * e

    def around(at, by, n):
        return lax.rem(at + (by + n), n)

    def remote(src, dst, send, recv, **to):
        return pltpu.make_async_remote_copy(
            src_ref=src, dst_ref=dst, send_sem=send, recv_sem=recv, device_id=to, device_id_type=MESH)

    def arrive(ref, sem):
        pltpu.make_async_copy(ref, ref, sem).wait()

    def span(q):
        return pl.ds(q * part, part)

    def side(q):
        return q * 2 // PIECES

    def token_copy():
        return pltpu.make_async_copy(tokens.at[e], hidden.at[1], in_sem.at[0])

    def weight(item, j):
        return {
            WK: lambda: wkv.at[j, :, :, pl.ds(0, HEAD)],
            WV: lambda: wkv.at[j, :, :, pl.ds(HEAD, HEAD)],
            WQ: lambda: wq.at[j],
            GAIN: lambda: gains.at[j],
            WO: lambda: wo.at[j],
            DOWN: lambda: down.at[j],
            UP: lambda: up.at[j],
        }[item]()

    sources = {WK: wk_hbm, WV: wv_hbm, WQ: wq_hbm, GAIN: gain_hbm, WO: wo_hbm}
    spare = {DOWN: down.at[2], UP: up.at[2]}

    def weight_copy(item):
        return remote({**sources, **spare}[item], weight(item, e), w_send.at[item], w_sem.at[e, item],
                      section=partner)

    small_copies = [
        pltpu.make_async_copy(qd_hbm, qd, small_sem.at[0]),
        pltpu.make_async_copy(vd_hbm, vd, small_sem.at[1]),
        pltpu.make_async_copy(tables.at[c], trig, small_sem.at[2]),
    ]

    @pl.when(first_pair)
    def _():
        token_copy().start()

    for copy in small_copies:
        copy.start()
    for item, source in sources.items():
        pltpu.make_async_copy(source, weight(item, e), w_sem.at[e, item]).start()

    barrier = pltpu.get_barrier_semaphore()
    neighbour = (around(z, 1, n_tp), around(z, -1, n_tp))
    peers = [{"tp": around(z, i, n_tp)} for i in range(1, n_tp)]
    peers += [{"ctx": around(c, i, n_ctx)} for i in range(1, n_ctx)]
    peers += [{"section": around(s, i, sections)} for i in range(1, sections)]
    peers += [{"section": around(s, 2, sections), "tp": neighbour[d]} for d in range(2)]
    for peer in peers:
        pl.semaphore_signal(barrier, 1, device_id=peer, device_id_type=MESH)

    for copy in small_copies:
        copy.wait()
    for slot, document in ((e, e), (2, 1 - e)):
        t = tenants[document]
        up[slot] = jnp.zeros(up.shape[1:], BF16)
        down[slot, :rank] = qd[t]
        down[slot, rank:] = vd[t]
        up[slot, :rank, :heads * HEAD] = q_up[t]
        up[slot, rank:, heads * HEAD:] = v_up[t]

    pl.semaphore_wait(barrier, len(peers))

    two_on = (around(z, 2, n_tp), around(z, -2, n_tp))

    def ag_copy(j, d, r, q, src):
        return remote(src.at[span(q)], agb.at[j, d, r, span(q)], ag_send.at[j, d, r, q],
                      ag_recv.at[j, d, r, q], tp=neighbour[d])

    def ag_far(j, q):
        d = side(q)
        return remote(agb.at[j, d, 1, span(q)], agf.at[j, span(q)], ag_send.at[j, d, FAR, q],
                      ag_recv.at[j, d, FAR, q], tp=two_on[d])

    def rs_copy(j, d, r, q):
        return remote(rso.at[j, d, r, span(q)], rsb.at[j, d, r, span(q)], rs_send.at[j, d, r, q],
                      rs_recv.at[j, d, r, q], tp=neighbour[d])

    def rs_far(j, q):
        d = side(q)
        return remote(rsfo.at[j, span(q)], rsf.at[j, span(q)], rs_send.at[j, d, FAR, q],
                      rs_recv.at[j, d, FAR, q], tp=two_on[d])

    def prt_copy(j, d, q):
        slot = jnp.where(j == 0, 1, jnp.where(last_pair, 2, 0))
        where = jnp.where((j == 1) & jnp.logical_not(last_pair), around(s, 2, sections), s)
        return remote(rso.at[j, d, 2, span(q)], prt.at[slot, d, span(q)], rs_send.at[j, d, 2, q],
                      prt_recv.at[slot, d, q], tp=neighbour[d], section=where)

    def pass_copy(buf, i):
        return remote(buf.at[2], buf.at[0], pass_send.at[i], pass_recv.at[i], section=around(s, 2, sections))

    def ctx_peer(dy, dx):
        across = n_ctx // 2
        return around(c // across, dy, 2) * across + around(lax.rem(c, across), dx, across)

    def kv_copy(j, offset):
        dy, dx = offset
        i = dy * (n_ctx // 2) + dx
        return remote(kvbuf.at[j, c], kvbuf.at[j, c], kv_send.at[j, i], kv_recv.at[j, i],
                      ctx=ctx_peer(dy, dx))

    def ss_copy(i):
        return remote(ssb.at[0], ssb.at[i], ss_send.at[i], ss_recv.at[i], tp=around(z, i, n_tp))

    def pp_copy(i):
        return remote(ppb.at[0], ppb.at[i], pp_send.at[i], pp_recv.at[i], ctx=around(c, i, n_ctx))

    def sq_copy(i):
        return remote(sqb.at[0], sqb.at[i], sq_send.at[i], sq_recv.at[i], tp=around(z, i, n_tp))

    def fin_copy(i):
        return remote(res.at[e], res.at[e], fin_send.at[i], fin_recv.at[e], section=around(s, i, sections))

    def rotate(x):
        return x * trig[0] + pltpu.roll(x, HEAD // 2, axis=1) * trig[1]

    def take(j, blocks, first=False):
        values = None
        for block, g in blocks:
            h = block.astype(F32)
            columns = pl.ds(pl.multiple_of(g * width, width), width)
            x = (h * gains[j, :, columns]).astype(BF16)
            new = (
                fold(h * h),
                jnp.dot(x, wkv[j, g], preferred_element_type=F32),
                lax.dot_general(x, down[j, :, columns], (((1,), (1,)), ((), ())), preferred_element_type=F32),
                jnp.dot(x, wq[j, g], preferred_element_type=F32),
            )
            values = new if values is None else [a + b for a, b in zip(values, new)]
        for ref, value in zip((squares, acc_kv, acc_l, acc_q), values):
            ref[...] = value if first else ref[...] + value

    def join(i, q):
        for d in range(2):
            arrive(prt.at[i, d, span(q)], prt_recv.at[i, d, q])
        at = slice(q * part, (q + 1) * part)
        sums = prt[i, 0, at].astype(F32) + prt[i, 1, at].astype(F32)
        hidden[i + 1, at] = (hidden[i, at].astype(F32) + own[i, at].astype(F32) + sums).astype(BF16)

    def layer(j, carry):
        @pl.when(first_pair & (j == 0))
        def _():
            token_copy().wait()

        @pl.when(jnp.logical_not(first_pair) & (j == 0))
        def _():
            arrive(hidden.at[0], pass_recv.at[0])
            arrive(own.at[0], pass_recv.at[1])

        for q in range(PIECES):
            @pl.when(jnp.logical_not(first_pair) | (j == 1))
            def _():
                join(j, q)

            for d in range(2):
                ag_copy(j, d, 0, q, hidden.at[j + 1]).start()

        @pl.when(j == 0)
        def _():
            for item in (GAIN, DOWN, UP, WK, WV, WQ):
                weight_copy(item).start()

        @pl.when((j == 1) & jnp.logical_not(last_pair))
        def _():
            pass_copy(hidden, 0).start()

        def own_take():
            for item in (GAIN, WK, WV, WQ):
                arrive(weight(item, j), w_sem.at[j, item])

            @pl.when(j != e)
            def _():
                for item in (DOWN, UP):
                    arrive(weight(item, j), w_sem.at[j, item])

            take(j, [(hidden[j + 1], z)], first=True)

        def pair_take(r):
            take(j, [(agb[j, d, r], around(z, -1 - r if d == 0 else 1 + r, n_tp)) for d in range(2)])

        late = first_pair & (e == 1) & (j == 0)
        prompt = jnp.logical_not(late)

        @pl.when(prompt)
        def _():
            own_take()

        for r in range(3):
            for q in range(PIECES):
                for d in range(2):
                    arrive(agb.at[j, d, r, span(q)], ag_recv.at[j, d, r, q])
                    if r < 2:
                        ag_copy(j, d, r + 1, q, agb.at[j, d, r]).start()
                    if r == 1 and d == side(q):
                        ag_far(j, q).start()

            @pl.when(prompt)
            def _():
                pair_take(r)

        @pl.when(j == 0)
        def _():
            weight_copy(WO).start()

        @pl.when(late)
        def _():
            own_take()

            def after(r, carry):
                pair_take(r)
                return carry

            lax.fori_loop(0, 3, after, 0)

        for q in range(PIECES):
            arrive(agf.at[j, span(q)], ag_recv.at[j, side(q), FAR, q])
        take(j, [(agf[j], around(z, 4, n_tp))])

        mean = jnp.sum(squares[...], axis=1, keepdims=True) * (1.0 / full_width)
        scale = lax.rsqrt(mean + 1e-5)
        low = (acc_l[...] * scale).astype(BF16)
        kv = acc_kv[...] * scale
        kvbuf[j, c, :, :HEAD] = rotate(kv[:, :HEAD]).astype(BF16)
        added = jnp.dot(low, up[j, :, heads * HEAD:], preferred_element_type=F32)
        kvbuf[j, c, :, HEAD:] = (kv[:, HEAD:] + added).astype(BF16)
        for offset in NEAR + REST:
            kv_copy(j, offset).start()
        factor = HEAD ** -0.5 * math.log2(math.e)
        for g in range(heads):
            cols = slice(g * HEAD, (g + 1) * HEAD)
            q = acc_q[:, cols] * scale + jnp.dot(low, up[j, :, cols], preferred_element_type=F32)
            qbuf[g] = (rotate(q) * factor).astype(BF16)

        n = lengths[e]
        lane = lax.broadcasted_iota(jnp.int32, (1, rows), 1)

        def keys_of(offsets):
            sources = [ctx_peer(-dy, -dx) for dy, dx in offsets]
            blocks = [kvbuf[j, source] for source in sources]
            valid = jnp.concatenate([lane + source * rows < n for source in sources], axis=1)
            return (jnp.concatenate([block[:, :HEAD] for block in blocks], axis=0),
                    jnp.concatenate([block[:, HEAD:] for block in blocks], axis=0), valid)

        def scored(g, keys, valid):
            scores = lax.dot_general(
                qbuf[g], keys, (((1,), (1,)), ((), ())), preferred_element_type=F32)
            return jnp.where(valid, scores, -1e30)

        for offset in NEAR:
            kv_copy(j, offset).wait_recv()
        keys, values, valid = keys_of(((0, 0),) + NEAR)
        near = []
        for g in range(heads):
            scores = scored(g, keys, valid)
            top = jnp.max(scores, axis=1, keepdims=True)
            weights = jnp.exp2(scores - top)
            total = jnp.sum(weights, axis=1, keepdims=True)
            near.append((top, total, jnp.dot(weights.astype(BF16), values, preferred_element_type=F32)))
        for offset in REST:
            kv_copy(j, offset).wait_recv()
        keys, values, valid = keys_of(REST)
        for g in range(heads):
            top_near, total_near, mixed_near = near[g]
            scores = scored(g, keys, valid)
            top = jnp.maximum(jnp.max(scores, axis=1, keepdims=True), top_near)
            weights = jnp.exp2(scores - top)
            fade = jnp.exp2(top_near - top)
            total = jnp.sum(weights, axis=1, keepdims=True) + total_near * fade
            mixed = jnp.dot(weights.astype(BF16), values, preferred_element_type=F32) + mixed_near * fade
            att[:, g * HEAD:(g + 1) * HEAD] = (mixed * (1.0 / total)).astype(BF16)

        arrive(weight(WO, j), w_sem.at[j, WO])

        def term(index):
            columns = pl.ds(pl.multiple_of(index * width, width), width)
            return jnp.dot(att[...], wo[j, :, columns], preferred_element_type=F32)

        def term_at(d, distance):
            return term(around(z, distance if d == 0 else -distance, n_tp))

        rsfo[j] = term_at(0, 4).astype(BF16)
        for q in range(PIECES):
            rs_far(j, q).start()
        for d in range(2):
            rso[j, d, 0] = term_at(d, 3).astype(BF16)
            for q in range(PIECES):
                rs_copy(j, d, 0, q).start()
        for d in range(2):
            terms[d] = term_at(d, 2)
        own[j + 1] = term(z).astype(BF16)

        @pl.when((j == 1) & jnp.logical_not(last_pair))
        def _():
            pass_copy(own, 1).start()

        for q in range(PIECES):
            at = slice(q * part, (q + 1) * part)
            for d in (side(q), 1 - side(q)):
                arrive(rsb.at[j, d, 0, span(q)], rs_recv.at[j, d, 0, q])
                value = terms[d, at] + rsb[j, d, 0, at].astype(F32)
                if d == side(q):
                    arrive(rsf.at[j, span(q)], rs_recv.at[j, d, FAR, q])
                    value = value + rsf[j, at].astype(F32)
                rso[j, d, 1, at] = value.astype(BF16)
                rs_copy(j, d, 1, q).start()
        for d in range(2):
            terms[d] = term_at(d, 1)
        for q in range(PIECES):
            at = slice(q * part, (q + 1) * part)
            for d in range(2):
                arrive(rsb.at[j, d, 1, span(q)], rs_recv.at[j, d, 1, q])
                rso[j, d, 2, at] = (terms[d, at] + rsb[j, d, 1, at].astype(F32)).astype(BF16)
                prt_copy(j, d, q).start()
        return carry

    lax.fori_loop(0, 2, layer, 0)

    @pl.when(last_pair)
    def _():
        for q in range(PIECES):
            join(2, q)
        wide = hidden[3].astype(F32)
        folded = fold(wide * wide)
        row = jnp.sum(jnp.transpose(folded), axis=0, keepdims=True)
        ssb[0] = jnp.broadcast_to(row, (8, rows))
        for i in range(1, n_tp):
            ss_copy(i).start()
        for i in range(1, n_tp):
            ss_copy(i).wait_recv()
        row = jnp.sum(ssb[...], axis=0)[:1]
        column = jnp.transpose(jnp.broadcast_to(row, (rows, rows)))[:, :1]
        scale = lax.rsqrt(column * (1.0 / full_width) + 1e-5)
        n = lengths[e]
        position = c * rows + lax.broadcasted_iota(jnp.int32, (rows, 1), 0)
        scale = jnp.where(position < n, scale, 0.0)
        pooled = jnp.sum(hidden[3].astype(F32) * scale, axis=0, keepdims=True)
        ppb[0] = jnp.broadcast_to(pooled * closing[...] / n.astype(F32), (8, width))
        for i in range(1, n_ctx):
            pp_copy(i).start()
        for i in range(1, n_ctx):
            pp_copy(i).wait_recv()
        pooled = jnp.sum(ppb[...], axis=0)
        sqb[0] = jnp.broadcast_to(jnp.sum(pooled * pooled, axis=1, keepdims=True), (8, HEAD))
        for i in range(1, n_tp):
            sq_copy(i).start()
        for i in range(1, n_tp):
            sq_copy(i).wait_recv()
        norms = jnp.sum(sqb[...], axis=0)[:, :1]
        res[e] = pooled * lax.rsqrt(norms * (1.0 / full_width) + 1e-6)
        for i in range(1, sections):
            fin_copy(i).start()
        arrive(res.at[1 - e], fin_recv.at[1 - e])
        for i in range(1, n_ctx):
            pp_copy(i).wait_send()
        for i in range(1, n_tp):
            sq_copy(i).wait_send()
            ss_copy(i).wait_send()
        for i in range(1, sections):
            fin_copy(i).wait_send()

    @pl.when(jnp.logical_not(last_pair))
    def _():
        pass_copy(hidden, 0).wait_send()
        pass_copy(own, 1).wait_send()
        for i in range(micro):
            arrive(res.at[i], fin_recv.at[i])

    for i in range(micro):
        out[i:i + 1] = res[i, :1]

    for item in range(7):
        weight_copy(item).wait_send()
    for j in range(2):
        for q in range(PIECES):
            for d in range(2):
                for r in range(3):
                    ag_copy(j, d, r, q, agb.at[j, d, r]).wait_send()
                for r in range(2):
                    rs_copy(j, d, r, q).wait_send()
                prt_copy(j, d, q).wait_send()
            ag_far(j, q).wait_send()
            rs_far(j, q).wait_send()
        for offset in NEAR + REST:
            kv_copy(j, offset).wait_send()


def build(mesh):
    sections, n_ctx, n_tp = (mesh.shape[a] for a in ("section", "ctx", "tp"))

    def shards(
        tokens, document_lengths, tenant_indices, attention_norm_gain, query_weight, key_weight,
        value_weight, output_weight, query_adapter_down, query_adapter_up, value_adapter_down,
        value_adapter_up, closing_norm_gain,
    ):
        micro, rows, width = tokens.shape
        query_width = query_weight.shape[2]
        tenant_count, rank = query_adapter_down.shape[1], query_adapter_down.shape[3]
        heads = query_width // HEAD

        freq = (500000.0 ** (-np.arange(HEAD // 2) / (HEAD // 2))).astype(np.float32)
        angle = np.arange(rows * n_ctx, dtype=np.float32)[:, None] * freq[None, :]
        cosine, sine = np.cos(angle.astype(np.float64)), np.sin(angle.astype(np.float64))
        tables = np.stack([np.concatenate([cosine, cosine], 1), np.concatenate([-sine, sine], 1)])
        tables = tables.reshape(2, n_ctx, rows, HEAD).transpose(1, 0, 2, 3).astype(np.float32)

        vmem = pl.BlockSpec(memory_space=pltpu.VMEM)
        hbm = pl.BlockSpec(memory_space=pl.ANY)
        smem = pl.BlockSpec(memory_space=pltpu.SMEM)
        dma = pltpu.SemaphoreType.DMA
        block = (rows, width)

        def body(*refs):
            kernel((sections, n_ctx, n_tp, micro, rows, width), *refs)

        return pl.pallas_call(
            body,
            out_shape=jax.ShapeDtypeStruct((micro, width), F32),
            in_specs=[smem, smem, hbm, hbm, vmem, hbm, hbm, hbm, hbm, hbm, hbm, hbm, vmem, vmem],
            out_specs=vmem,
            scratch_shapes=[
                pltpu.VMEM((2, n_tp, width, query_width), BF16),
                pltpu.VMEM((2, n_tp, width, 2 * HEAD), BF16),
                pltpu.VMEM((2, query_width, width * n_tp), BF16),
                pltpu.VMEM((2, 1, width * n_tp), F32),
                pltpu.VMEM((tenant_count, rank, width * n_tp), BF16),
                pltpu.VMEM((tenant_count, rank, width * n_tp), BF16),
                pltpu.VMEM((3, 2 * rank, width * n_tp), BF16),
                pltpu.VMEM((3, 2 * rank, query_width + HEAD), BF16),
                pltpu.VMEM((2, rows, HEAD), F32),
                pltpu.VMEM((4,) + block, BF16),
                pltpu.VMEM((3,) + block, BF16),
                pltpu.VMEM((2, 2, 3) + block, BF16),
                pltpu.VMEM((2,) + block, BF16),
                pltpu.VMEM((2, 2, 2) + block, BF16),
                pltpu.VMEM((2,) + block, BF16),
                pltpu.VMEM((2, 2, 3) + block, BF16),
                pltpu.VMEM((2,) + block, BF16),
                pltpu.VMEM((3, 2) + block, BF16),
                pltpu.VMEM((2, n_ctx, rows, 2 * HEAD), BF16),
                pltpu.VMEM((rows, query_width), F32),
                pltpu.VMEM((rows, 2 * HEAD), F32),
                pltpu.VMEM((rows, 2 * rank), F32),
                pltpu.VMEM((rows, HEAD), F32),
                pltpu.VMEM((heads, rows, HEAD), BF16),
                pltpu.VMEM((rows, query_width), BF16),
                pltpu.VMEM((2,) + block, F32),
                pltpu.VMEM((n_tp, 8, rows), F32),
                pltpu.VMEM((n_ctx, 8, width), F32),
                pltpu.VMEM((n_tp, 8, HEAD), F32),
                pltpu.VMEM((micro, 8, width), F32),
                dma((2, 7)),
                dma((7,)),
                dma((3,)),
                dma((1,)),
                dma((2, 2, 4, PIECES)),
                dma((2, 2, 4, PIECES)),
                dma((2, 2, 4, PIECES)),
                dma((2, 2, 4, PIECES)),
                dma((3, 2, PIECES)),
                dma((2, n_ctx)),
                dma((2, n_ctx)),
                dma((2,)),
                dma((2,)),
                dma((n_tp,)),
                dma((n_tp,)),
                dma((n_ctx,)),
                dma((n_ctx,)),
                dma((n_tp,)),
                dma((n_tp,)),
                dma((sections,)),
                dma((micro,)),
            ],
            compiler_params=pltpu.CompilerParams(
                collective_id=0, has_side_effects=True, vmem_limit_bytes=60 << 20),
            cost_estimate=pl.CostEstimate(
                flops=micro * 2 * rows * (n_tp * width * (query_width + 3 * HEAD) * 2),
                bytes_accessed=16 << 20, transcendentals=micro * heads * rows * rows * n_ctx),
        )(
            document_lengths, tenant_indices, tokens, attention_norm_gain,
            closing_norm_gain.reshape(1, width), jnp.asarray(tables),
            query_weight.reshape(n_tp, width, query_width),
            key_weight.reshape(n_tp, width, HEAD), value_weight.reshape(n_tp, width, HEAD),
            output_weight[0],
            jnp.swapaxes(query_adapter_down[0], 1, 2), jnp.swapaxes(value_adapter_down[0], 1, 2),
            query_adapter_up[0], value_adapter_up[0],
        )

    return shards


def solution(mesh):
    placed = (
        P(None, "ctx", "tp"),
        P(),
        P(),
        P("section", None),
        P("section", None, "tp"),
        P("section", None, "tp"),
        P("section", None, "tp"),
        P("section", "tp", None),
        P("section", None, None, None),
        P("section", None, None, "tp"),
        P("section", None, None, None),
        P("section", None, None, "tp"),
        P("tp"),
    )
    return jax.shard_map(
        build(mesh), mesh=mesh, in_specs=placed, out_specs=P(None, "tp"), check_vma=False
    )
```

time: 853 us -> 190 us (0.22)
  waiting for transfers between devices: 388 us -> 0 us
  blocking collectives: 291 us -> 0 us
  Pallas kernels: 0 us -> 189 us
  matrix products: 66.3 us -> 0 us
  starting transfers between devices: 39.9 us -> 0 us
  other arithmetic: 26.5 us -> 0 us
  between operations: 24 us -> 0.01 us
    reduce_scatter x5 -> x0, waiting for transfers between devices: 224 us -> none  [shards(): lax.psum_scatter(jnp.dot(mixed, out_rows, preferred_element_type=jnp.floa...]
    all_gather x10 -> x0, blocking collectives: 200 us -> none  [the longest x5 101 us: shards(): keys = lax.all_gather(key, 'ctx', axis=0, tiled=True)]
    pallas_call x0 -> x1, Pallas kernels: none -> 189 us  [shards(): pl.pallas_call(body, out_shape=jax.ShapeDtypeStruct((micro, width), F32),...]
    all_gather x5 -> x0, waiting for transfers between devices: 156 us -> none  [shards(): whole = lax.all_gather(current, 'tp', axis=1, tiled=True)]
    psum x3 -> x0, blocking collectives: 91.3 us -> none  [the longest x1 68.1 us: shards(): lax.psum(jnp.where(section == sections - 1, partial_value, 0.0), ('sectio...]
    dot_general x40 -> x0, matrix products: 66.3 us -> none  [the longest x5 15.5 us: shards(): jnp.dot(normalized_state, query_weight[0], preferred_element_type=jnp.flo...]
    ppermute x4 -> x0, starting transfers between devices: 39.5 us -> none  [shifted(): return lax.ppermute(array, axis, pairs)]
    reduce_sum x13 -> x0, other arithmetic: 11 us -> none  [the longest x5 8.03 us: rms_scale(): jnp.mean(values * values, axis=-1, keepdims=True) + epsilon]
  transfers between devices with their start and end apart: 14 -> 0, of which waited for: 14 -> 0; matrix products, arithmetic and copies ran while one was open for 1% -> 0% of each run, Pallas kernels for 0% -> 0%
where the time goes in v1:
time: 190 us
  Pallas kernels  189 us (99%)
    pallas_call x1, Pallas kernels, shards(): pl.pallas_call(body, out_shape=jax.ShapeDtypeStruct((micro, width), F32),...  189 us

profile of v1, /device:TPU:1, one launch (start us, length us, event | category | flops | bytes accessed | tf_op | source)
XLA Modules:
  0.0 190.3 jit_solution(3738348311833625111)
XLA Ops:
  0.0 189.0 %shard_map.136 = f32[2,512]{1,0:T(2,128)} custom-call(s32[2]{0:T(128)} %refs_0_.1, s32[2]{0:T(128)} %refs_1_.1, bf16[2,128,512]{2,1,0:T(8,128)(2,1)} %refs_2_.1, f32[1,4096]{1,0:T(1,128)} %refs_3_.1, f32[1,512]{1,0:T(1,128)} %bitcast.21, f32[8,2,128,128]{3,2,1,0:T(8,128)} %constant.2.clone.refs_5_, bf16[8,512,512]{2,1,0:T(8,128)(2,1)} %bitcast.13, ...), custom_call_target="tpu_custom_call" | custom-call | flops 3758096384 | bytes 16777216 | tf_op jit(solution)/shard_map/pallas_call | solution.py:481
  189.0 1.3 copy.16

commit v2 on v1

--- a/solution.py
+++ b/solution.py
@@ -13,7 +13,7 @@
 BF16 = jnp.bfloat16
 MESH = pl.DeviceIdType.MESH
 
-PIECES = 2
+PIECES = 4
 FAR = 3
 WK, WV, WQ, GAIN, WO, DOWN, UP = range(7)
 NEAR = ((1, 0), (0, 1), (0, 3))

time: 190 us -> 181 us (0.953)
  Pallas kernels: 189 us -> 180 us
    pallas_call x1, Pallas kernels: 189 us -> 180 us  [shards(): pl.pallas_call(body, out_shape=jax.ShapeDtypeStruct((micro, width), F32),...]
where the time goes in v2:
time: 181 us
  Pallas kernels  180 us (99%)
    pallas_call x1, Pallas kernels, shards(): pl.pallas_call(body, out_shape=jax.ShapeDtypeStruct((micro, width), F32),...  180 us

profile of v2, /device:TPU:1, one launch (start us, length us, event | category | flops | bytes accessed | tf_op | source)
XLA Modules:
  0.0 181.1 jit_solution(813916044331818458)
XLA Ops:
  0.0 179.9 %shard_map.136 = f32[2,512]{1,0:T(2,128)} custom-call(s32[2]{0:T(128)} %refs_0_.1, s32[2]{0:T(128)} %refs_1_.1, bf16[2,128,512]{2,1,0:T(8,128)(2,1)} %refs_2_.1, f32[1,4096]{1,0:T(1,128)} %refs_3_.1, f32[1,512]{1,0:T(1,128)} %bitcast.21, f32[8,2,128,128]{3,2,1,0:T(8,128)} %constant.2.clone.refs_5_, bf16[8,512,512]{2,1,0:T(8,128)(2,1)} %bitcast.13, ...), custom_call_target="tpu_custom_call" | custom-call | flops 3758096384 | bytes 16777216 | tf_op jit(solution)/shard_map/pallas_call | solution.py:481
  179.9 1.3 copy.16

commit v3 on v2

--- a/solution.py
+++ b/solution.py
@@ -33,12 +33,12 @@
     qd_hbm, vd_hbm, q_up, v_up,
     out,
     wq, wkv, wo, gains, qd, vd, down, up, trig,
-    hidden, own, agb, agf, rsb, rsf, rso, rsfo, prt, kvbuf,
+    hidden, own, agb, agf, rsb, rsf, rso, rsfo, prt, kvbuf, mirror,
     acc_q, acc_kv, acc_l, squares, qbuf, att, terms,
     ssb, ppb, sqb, res,
     w_sem, w_send, small_sem, in_sem, ag_send, ag_recv, rs_send, rs_recv, prt_recv,
     kv_send, kv_recv, pass_send, pass_recv, ss_send, ss_recv, pp_send, pp_recv, sq_send, sq_recv,
-    fin_send, fin_recv,
+    fin_send, fin_recv, mir_send, mir_recv, acc_send, acc_recv,
 ):
     sections, n_ctx, n_tp, micro, rows, width = sizes
     full_width = width * n_tp
@@ -52,6 +52,7 @@
     first_pair = s < 2
     last_pair = s >= sections - 2
     partner = s + 1 - 2 * e
+    helps = first_pair & (e == 0)
 
     def around(at, by, n):
         return lax.rem(at + (by + n), n)
@@ -177,10 +178,17 @@
     def fin_copy(i):
         return remote(res.at[e], res.at[e], fin_send.at[i], fin_recv.at[e], section=around(s, i, sections))
 
+    def mir_copy(slot, block):
+        return remote(block, mirror.at[slot], mir_send.at[slot], mir_recv.at[slot], section=partner)
+
+    def acc_copy(i):
+        ref = (squares, acc_kv, acc_l, acc_q)[i]
+        return remote(ref.at[1], ref.at[0], acc_send.at[i], acc_recv.at[i], section=partner)
+
     def rotate(x):
         return x * trig[0] + pltpu.roll(x, HEAD // 2, axis=1) * trig[1]
 
-    def take(j, blocks, first=False):
+    def take(j, blocks, first=False, to=0, adapter=None):
         values = None
         for block, g in blocks:
             h = block.astype(F32)
@@ -189,12 +197,12 @@
             new = (
                 fold(h * h),
                 jnp.dot(x, wkv[j, g], preferred_element_type=F32),
-                lax.dot_general(x, down[j, :, columns], (((1,), (1,)), ((), ())), preferred_element_type=F32),
+                lax.dot_general(x, down[j if adapter is None else adapter, :, columns], (((1,), (1,)), ((), ())), preferred_element_type=F32),
                 jnp.dot(x, wq[j, g], preferred_element_type=F32),
             )
             values = new if values is None else [a + b for a, b in zip(values, new)]
         for ref, value in zip((squares, acc_kv, acc_l, acc_q), values):
-            ref[...] = value if first else ref[...] + value
+            ref[to] = value if first else ref[to] + value
 
     def join(i, q):
         for d in range(2):
@@ -223,8 +231,12 @@
 
         @pl.when(j == 0)
         def _():
-            for item in (GAIN, DOWN, UP, WK, WV, WQ):
-                weight_copy(item).start()
+            weight_copy(UP).start()
+
+            @pl.when(jnp.logical_not(helps))
+            def _():
+                for item in (GAIN, DOWN, WK, WV, WQ):
+                    weight_copy(item).start()
 
         @pl.when((j == 1) & jnp.logical_not(last_pair))
         def _():
@@ -241,8 +253,8 @@
 
             take(j, [(hidden[j + 1], z)], first=True)
 
-        def pair_take(r):
-            take(j, [(agb[j, d, r], around(z, -1 - r if d == 0 else 1 + r, n_tp)) for d in range(2)])
+        def owner(d, r):
+            return around(z, -1 - r if d == 0 else 1 + r, n_tp)
 
         late = first_pair & (e == 1) & (j == 0)
         prompt = jnp.logical_not(late)
@@ -250,6 +262,10 @@
         @pl.when(prompt)
         def _():
             own_take()
+
+        @pl.when(late)
+        def _():
+            mir_copy(0, hidden.at[1]).start()
 
         for r in range(3):
             for q in range(PIECES):
@@ -262,39 +278,57 @@
 
             @pl.when(prompt)
             def _():
-                pair_take(r)
+                take(j, [(agb[j, d, r], owner(d, r)) for d in range(2)])
+
+            @pl.when(late)
+            def _():
+                for d in range(2):
+                    mir_copy(1 + 2 * r + d, agb.at[j, d, r]).start()
 
         @pl.when(j == 0)
         def _():
             weight_copy(WO).start()
-
-        @pl.when(late)
-        def _():
-            own_take()
-
-            def after(r, carry):
-                pair_take(r)
-                return carry
-
-            lax.fori_loop(0, 3, after, 0)
 
         for q in range(PIECES):
             arrive(agf.at[j, span(q)], ag_recv.at[j, side(q), FAR, q])
-        take(j, [(agf[j], around(z, 4, n_tp))])
-
-        mean = jnp.sum(squares[...], axis=1, keepdims=True) * (1.0 / full_width)
+
+        @pl.when(prompt)
+        def _():
+            take(j, [(agf[j], around(z, 4, n_tp))])
+
+        @pl.when(late)
+        def _():
+            mir_copy(7, agf.at[j]).start()
+            arrive(weight(UP, 0), w_sem.at[0, UP])
+            for i, ref in enumerate((squares, acc_kv, acc_l, acc_q)):
+                arrive(ref.at[0], acc_recv.at[i])
+
+        mean = jnp.sum(squares[0], axis=1, keepdims=True) * (1.0 / full_width)
         scale = lax.rsqrt(mean + 1e-5)
-        low = (acc_l[...] * scale).astype(BF16)
-        kv = acc_kv[...] * scale
-        kvbuf[j, c, :, :HEAD] = rotate(kv[:, :HEAD]).astype(BF16)
+        low = (acc_l[0] * scale).astype(BF16)
+        kv = acc_kv[0] * scale
+        kvbuf[j, c, :, :HEAD] = jnp.transpose(rotate(kv[:, :HEAD])).astype(BF16)
         added = jnp.dot(low, up[j, :, heads * HEAD:], preferred_element_type=F32)
         kvbuf[j, c, :, HEAD:] = (kv[:, HEAD:] + added).astype(BF16)
         for offset in NEAR + REST:
             kv_copy(j, offset).start()
+
+        @pl.when(helps & (j == 0))
+        def _():
+            for slots in ((0,), (1, 2), (3, 4), (5, 6), (7,)):
+                for slot in slots:
+                    arrive(mirror.at[slot], mir_recv.at[slot])
+                owners = [z if slot == 0 else around(z, 4, n_tp) if slot == 7
+                          else owner((slot - 1) % 2, (slot - 1) // 2) for slot in slots]
+                take(0, [(mirror[slot], at) for slot, at in zip(slots, owners)],
+                     first=slots == (0,), to=1, adapter=2)
+            for i in range(4):
+                acc_copy(i).start()
+
         factor = HEAD ** -0.5 * math.log2(math.e)
         for g in range(heads):
             cols = slice(g * HEAD, (g + 1) * HEAD)
-            q = acc_q[:, cols] * scale + jnp.dot(low, up[j, :, cols], preferred_element_type=F32)
+            q = acc_q[0, :, cols] * scale + jnp.dot(low, up[j, :, cols], preferred_element_type=F32)
             qbuf[g] = (rotate(q) * factor).astype(BF16)
 
         n = lengths[e]
@@ -304,12 +338,11 @@
             sources = [ctx_peer(-dy, -dx) for dy, dx in offsets]
             blocks = [kvbuf[j, source] for source in sources]
             valid = jnp.concatenate([lane + source * rows < n for source in sources], axis=1)
-            return (jnp.concatenate([block[:, :HEAD] for block in blocks], axis=0),
+            return (jnp.concatenate([block[:, :HEAD] for block in blocks], axis=1),
                     jnp.concatenate([block[:, HEAD:] for block in blocks], axis=0), valid)
 
         def scored(g, keys, valid):
-            scores = lax.dot_general(
-                qbuf[g], keys, (((1,), (1,)), ((), ())), preferred_element_type=F32)
+            scores = jnp.dot(qbuf[g], keys, preferred_element_type=F32)
             return jnp.where(valid, scores, -1e30)
 
         for offset in NEAR:
@@ -434,8 +467,24 @@
     for i in range(micro):
         out[i:i + 1] = res[i, :1]
 
-    for item in range(7):
+    for item in (WO, UP):
         weight_copy(item).wait_send()
+
+    @pl.when(jnp.logical_not(helps))
+    def _():
+        for item in (WK, WV, WQ, GAIN, DOWN):
+            weight_copy(item).wait_send()
+
+    @pl.when(helps)
+    def _():
+        for i in range(4):
+            acc_copy(i).wait_send()
+
+    @pl.when(first_pair & (e == 1))
+    def _():
+        for slot in range(8):
+            mir_copy(slot, agf.at[0]).wait_send()
+
     for j in range(2):
         for q in range(PIECES):
             for d in range(2):
@@ -503,10 +552,11 @@
                 pltpu.VMEM((2,) + block, BF16),
                 pltpu.VMEM((3, 2) + block, BF16),
                 pltpu.VMEM((2, n_ctx, rows, 2 * HEAD), BF16),
-                pltpu.VMEM((rows, query_width), F32),
-                pltpu.VMEM((rows, 2 * HEAD), F32),
-                pltpu.VMEM((rows, 2 * rank), F32),
-                pltpu.VMEM((rows, HEAD), F32),
+                pltpu.VMEM((8,) + block, BF16),
+                pltpu.VMEM((2, rows, query_width), F32),
+                pltpu.VMEM((2, rows, 2 * HEAD), F32),
+                pltpu.VMEM((2, rows, 2 * rank), F32),
+                pltpu.VMEM((2, rows, HEAD), F32),
                 pltpu.VMEM((heads, rows, HEAD), BF16),
                 pltpu.VMEM((rows, query_width), BF16),
                 pltpu.VMEM((2,) + block, F32),
@@ -535,6 +585,10 @@
                 dma((n_tp,)),
                 dma((sections,)),
                 dma((micro,)),
+                dma((8,)),
+                dma((8,)),
+                dma((4,)),
+                dma((4,)),
             ],
             compiler_params=pltpu.CompilerParams(
                 collective_id=0, has_side_effects=True, vmem_limit_bytes=60 << 20),

time: 181 us -> 184 us (1.017)
  Pallas kernels: 180 us -> 183 us
    pallas_call x1, Pallas kernels: 180 us -> 183 us  [shards(): pl.pallas_call(body, out_shape=jax.ShapeDtypeStruct((micro, width), F32),...]
where the time goes in v3:
time: 184 us
  Pallas kernels  183 us (99%)
    pallas_call x1, Pallas kernels, shards(): pl.pallas_call(body, out_shape=jax.ShapeDtypeStruct((micro, width), F32),...  183 us

profile of v3, /device:TPU:1, one launch (start us, length us, event | category | flops | bytes accessed | tf_op | source)
XLA Modules:
  0.0 184.1 jit_solution(3387924111986555163)
XLA Ops:
  0.0 182.8 %shard_map.136 = f32[2,512]{1,0:T(2,128)} custom-call(s32[2]{0:T(128)} %refs_0_.1, s32[2]{0:T(128)} %refs_1_.1, bf16[2,128,512]{2,1,0:T(8,128)(2,1)} %refs_2_.1, f32[1,4096]{1,0:T(1,128)} %refs_3_.1, f32[1,512]{1,0:T(1,128)} %bitcast.21, f32[8,2,128,128]{3,2,1,0:T(8,128)} %constant.2.clone.refs_5_, bf16[8,512,512]{2,1,0:T(8,128)(2,1)} %bitcast.13, ...), custom_call_target="tpu_custom_call" | custom-call | flops 3758096384 | bytes 16777216 | tf_op jit(solution)/shard_map/pallas_call | solution.py:530
  182.8 1.3 copy.16

commit v4 on v2

--- a/solution.py
+++ b/solution.py
@@ -221,7 +221,7 @@
             for d in range(2):
                 ag_copy(j, d, 0, q, hidden.at[j + 1]).start()
 
-        @pl.when(j == 0)
+        @pl.when(first_pair & (j == 0))
         def _():
             for item in (GAIN, DOWN, UP, WK, WV, WQ):
                 weight_copy(item).start()
@@ -264,7 +264,7 @@
             def _():
                 pair_take(r)
 
-        @pl.when(j == 0)
+        @pl.when(first_pair & (j == 0))
         def _():
             weight_copy(WO).start()
 
@@ -378,6 +378,11 @@
                 rso[j, d, 2, at] = (terms[d, at] + rsb[j, d, 1, at].astype(F32)).astype(BF16)
                 prt_copy(j, d, q).start()
         return carry
+
+    @pl.when(jnp.logical_not(first_pair))
+    def _():
+        for item in (GAIN, DOWN, UP, WK, WV, WQ, WO):
+            weight_copy(item).start()
 
     lax.fori_loop(0, 2, layer, 0)
 

time: 181 us -> 182 us (level)
  no operation moved by 1% of the time
where the time goes in v4:
time: 182 us
  Pallas kernels  181 us (99%)
    pallas_call x1, Pallas kernels, shards(): pl.pallas_call(body, out_shape=jax.ShapeDtypeStruct((micro, width), F32),...  181 us

profile of v4, /device:TPU:1, one launch (start us, length us, event | category | flops | bytes accessed | tf_op | source)
XLA Modules:
  0.0 182.2 jit_solution(8089344399498678725)
XLA Ops:
  0.0 181.0 %shard_map.136 = f32[2,512]{1,0:T(2,128)} custom-call(s32[2]{0:T(128)} %refs_0_.1, s32[2]{0:T(128)} %refs_1_.1, bf16[2,128,512]{2,1,0:T(8,128)(2,1)} %refs_2_.1, f32[1,4096]{1,0:T(1,128)} %refs_3_.1, f32[1,512]{1,0:T(1,128)} %bitcast.21, f32[8,2,128,128]{3,2,1,0:T(8,128)} %constant.2.clone.refs_5_, bf16[8,512,512]{2,1,0:T(8,128)(2,1)} %bitcast.13, ...), custom_call_target="tpu_custom_call" | custom-call | flops 3758096384 | bytes 16777216 | tf_op jit(solution)/shard_map/pallas_call | solution.py:486
  181.0 1.3 copy.16

commit v5 on v4

--- a/solution.py
+++ b/solution.py
@@ -37,7 +37,7 @@
     acc_q, acc_kv, acc_l, squares, qbuf, att, terms,
     ssb, ppb, sqb, res,
     w_sem, w_send, small_sem, in_sem, ag_send, ag_recv, rs_send, rs_recv, prt_recv,
-    kv_send, kv_recv, pass_send, pass_recv, ss_send, ss_recv, pp_send, pp_recv, sq_send, sq_recv,
+    kv_send, kv_recv, pass_send, pass_recv, few_send, few_recv,
     fin_send, fin_recv,
 ):
     sections, n_ctx, n_tp, micro, rows, width = sizes
@@ -56,9 +56,10 @@
     def around(at, by, n):
         return lax.rem(at + (by + n), n)
 
-    def remote(src, dst, send, recv, **to):
+    def remote(src, dst, send, recv, section=s, ctx=c, tp=z):
         return pltpu.make_async_remote_copy(
-            src_ref=src, dst_ref=dst, send_sem=send, recv_sem=recv, device_id=to, device_id_type=MESH)
+            src_ref=src, dst_ref=dst, send_sem=send, recv_sem=recv, device_id=(section, ctx, tp),
+            device_id_type=MESH)
 
     def arrive(ref, sem):
         pltpu.make_async_copy(ref, ref, sem).wait()
@@ -107,10 +108,10 @@
 
     barrier = pltpu.get_barrier_semaphore()
     neighbour = (around(z, 1, n_tp), around(z, -1, n_tp))
-    peers = [{"tp": around(z, i, n_tp)} for i in range(1, n_tp)]
-    peers += [{"ctx": around(c, i, n_ctx)} for i in range(1, n_ctx)]
-    peers += [{"section": around(s, i, sections)} for i in range(1, sections)]
-    peers += [{"section": around(s, 2, sections), "tp": neighbour[d]} for d in range(2)]
+    peers = [(s, c, around(z, i, n_tp)) for i in range(1, n_tp)]
+    peers += [(s, around(c, i, n_ctx), z) for i in range(1, n_ctx)]
+    peers += [(around(s, i, sections), c, z) for i in range(1, sections)]
+    peers += [(around(s, 2, sections), c, neighbour[d]) for d in range(2)]
     for peer in peers:
         pl.semaphore_signal(barrier, 1, device_id=peer, device_id_type=MESH)
 
@@ -129,27 +130,27 @@
     two_on = (around(z, 2, n_tp), around(z, -2, n_tp))
 
     def ag_copy(j, d, r, q, src):
-        return remote(src.at[span(q)], agb.at[j, d, r, span(q)], ag_send.at[j, d, r, q],
-                      ag_recv.at[j, d, r, q], tp=neighbour[d])
+        return remote(src.at[span(q)], agb.at[j, d, r, span(q)], ag_send.at[j, 0],
+                      ag_recv.at[j, d, r, q if r < 2 else 0], tp=neighbour[d])
 
     def ag_far(j, q):
         d = side(q)
-        return remote(agb.at[j, d, 1, span(q)], agf.at[j, span(q)], ag_send.at[j, d, FAR, q],
-                      ag_recv.at[j, d, FAR, q], tp=two_on[d])
+        return remote(agb.at[j, d, 1, span(q)], agf.at[j, span(q)], ag_send.at[j, 1],
+                      ag_recv.at[j, 0, FAR, 0], tp=two_on[d])
 
     def rs_copy(j, d, r, q):
-        return remote(rso.at[j, d, r, span(q)], rsb.at[j, d, r, span(q)], rs_send.at[j, d, r, q],
+        return remote(rso.at[j, d, r, span(q)], rsb.at[j, d, r, span(q)], rs_send.at[j, 0],
                       rs_recv.at[j, d, r, q], tp=neighbour[d])
 
     def rs_far(j, q):
         d = side(q)
-        return remote(rsfo.at[j, span(q)], rsf.at[j, span(q)], rs_send.at[j, d, FAR, q],
+        return remote(rsfo.at[j, span(q)], rsf.at[j, span(q)], rs_send.at[j, 1],
                       rs_recv.at[j, d, FAR, q], tp=two_on[d])
 
     def prt_copy(j, d, q):
         slot = jnp.where(j == 0, 1, jnp.where(last_pair, 2, 0))
         where = jnp.where((j == 1) & jnp.logical_not(last_pair), around(s, 2, sections), s)
-        return remote(rso.at[j, d, 2, span(q)], prt.at[slot, d, span(q)], rs_send.at[j, d, 2, q],
+        return remote(rso.at[j, d, 2, span(q)], prt.at[slot, d, span(q)], rs_send.at[j, 0],
                       prt_recv.at[slot, d, q], tp=neighbour[d], section=where)
 
     def pass_copy(buf, i):
@@ -159,20 +160,20 @@
         across = n_ctx // 2
         return around(c // across, dy, 2) * across + around(lax.rem(c, across), dx, across)
 
+    ctx_ids = {offset: ctx_peer(*offset) for offset in NEAR + REST}
+
     def kv_copy(j, offset):
-        dy, dx = offset
-        i = dy * (n_ctx // 2) + dx
-        return remote(kvbuf.at[j, c], kvbuf.at[j, c], kv_send.at[j, i], kv_recv.at[j, i],
-                      ctx=ctx_peer(dy, dx))
+        return remote(kvbuf.at[j, c], kvbuf.at[j, c], kv_send.at[j],
+                      kv_recv.at[j, 0 if offset in NEAR else 1], ctx=ctx_ids[offset])
 
     def ss_copy(i):
-        return remote(ssb.at[0], ssb.at[i], ss_send.at[i], ss_recv.at[i], tp=around(z, i, n_tp))
+        return remote(ssb.at[0], ssb.at[i], few_send.at[0], few_recv.at[0], tp=around(z, i, n_tp))
 
     def pp_copy(i):
-        return remote(ppb.at[0], ppb.at[i], pp_send.at[i], pp_recv.at[i], ctx=around(c, i, n_ctx))
+        return remote(ppb.at[0], ppb.at[i], few_send.at[1], few_recv.at[1], ctx=around(c, i, n_ctx))
 
     def sq_copy(i):
-        return remote(sqb.at[0], sqb.at[i], sq_send.at[i], sq_recv.at[i], tp=around(z, i, n_tp))
+        return remote(sqb.at[0], sqb.at[i], few_send.at[2], few_recv.at[2], tp=around(z, i, n_tp))
 
     def fin_copy(i):
         return remote(res.at[e], res.at[e], fin_send.at[i], fin_recv.at[e], section=around(s, i, sections))
@@ -180,20 +181,25 @@
     def rotate(x):
         return x * trig[0] + pltpu.roll(x, HEAD // 2, axis=1) * trig[1]
 
-    def take(j, blocks, first=False):
+    def take(j, blocks, first=False, queries=True, others=True):
         values = None
         for block, g in blocks:
             h = block.astype(F32)
             columns = pl.ds(pl.multiple_of(g * width, width), width)
             x = (h * gains[j, :, columns]).astype(BF16)
-            new = (
-                fold(h * h),
-                jnp.dot(x, wkv[j, g], preferred_element_type=F32),
-                lax.dot_general(x, down[j, :, columns], (((1,), (1,)), ((), ())), preferred_element_type=F32),
-                jnp.dot(x, wq[j, g], preferred_element_type=F32),
-            )
+            new = []
+            if others:
+                new += [
+                    fold(h * h),
+                    jnp.dot(x, wkv[j, g], preferred_element_type=F32),
+                    lax.dot_general(
+                        x, down[j, :, columns], (((1,), (1,)), ((), ())), preferred_element_type=F32),
+                ]
+            if queries:
+                new.append(jnp.dot(x, wq[j, g], preferred_element_type=F32))
             values = new if values is None else [a + b for a, b in zip(values, new)]
-        for ref, value in zip((squares, acc_kv, acc_l, acc_q), values):
+        refs = ((squares, acc_kv, acc_l) if others else ()) + ((acc_q,) if queries else ())
+        for ref, value in zip(refs, values):
             ref[...] = value if first else ref[...] + value
 
     def join(i, q):
@@ -241,8 +247,8 @@
 
             take(j, [(hidden[j + 1], z)], first=True)
 
-        def pair_take(r):
-            take(j, [(agb[j, d, r], around(z, -1 - r if d == 0 else 1 + r, n_tp)) for d in range(2)])
+        def pair(r):
+            return [(agb[j, d, r], around(z, -1 - r if d == 0 else 1 + r, n_tp)) for d in range(2)]
 
         late = first_pair & (e == 1) & (j == 0)
         prompt = jnp.logical_not(late)
@@ -251,18 +257,17 @@
         def _():
             own_take()
 
-        for r in range(3):
+        for r in range(2):
             for q in range(PIECES):
                 for d in range(2):
                     arrive(agb.at[j, d, r, span(q)], ag_recv.at[j, d, r, q])
-                    if r < 2:
-                        ag_copy(j, d, r + 1, q, agb.at[j, d, r]).start()
+                    ag_copy(j, d, r + 1, q, agb.at[j, d, r]).start()
                     if r == 1 and d == side(q):
                         ag_far(j, q).start()
 
             @pl.when(prompt)
             def _():
-                pair_take(r)
+                take(j, pair(r))
 
         @pl.when(first_pair & (j == 0))
         def _():
@@ -271,16 +276,15 @@
         @pl.when(late)
         def _():
             own_take()
-
-            def after(r, carry):
-                pair_take(r)
-                return carry
-
-            lax.fori_loop(0, 3, after, 0)
-
-        for q in range(PIECES):
-            arrive(agf.at[j, span(q)], ag_recv.at[j, side(q), FAR, q])
-        take(j, [(agf[j], around(z, 4, n_tp))])
+            for r in range(2):
+                take(j, pair(r))
+
+        for d in range(2):
+            arrive(agb.at[j, d, 2], ag_recv.at[j, d, 2, 0])
+        take(j, pair(2), queries=False)
+        arrive(agf.at[j], ag_recv.at[j, 0, FAR, 0])
+        far = [(agf[j], around(z, 4, n_tp))]
+        take(j, far, queries=False)
 
         mean = jnp.sum(squares[...], axis=1, keepdims=True) * (1.0 / full_width)
         scale = lax.rsqrt(mean + 1e-5)
@@ -291,6 +295,7 @@
         kvbuf[j, c, :, HEAD:] = (kv[:, HEAD:] + added).astype(BF16)
         for offset in NEAR + REST:
             kv_copy(j, offset).start()
+        take(j, pair(2) + far, others=False)
         factor = HEAD ** -0.5 * math.log2(math.e)
         for g in range(heads):
             cols = slice(g * HEAD, (g + 1) * HEAD)
@@ -312,8 +317,7 @@
                 qbuf[g], keys, (((1,), (1,)), ((), ())), preferred_element_type=F32)
             return jnp.where(valid, scores, -1e30)
 
-        for offset in NEAR:
-            kv_copy(j, offset).wait_recv()
+        arrive(kvbuf.at[j, pl.ds(0, len(NEAR))], kv_recv.at[j, 0])
         keys, values, valid = keys_of(((0, 0),) + NEAR)
         near = []
         for g in range(heads):
@@ -322,8 +326,7 @@
             weights = jnp.exp2(scores - top)
             total = jnp.sum(weights, axis=1, keepdims=True)
             near.append((top, total, jnp.dot(weights.astype(BF16), values, preferred_element_type=F32)))
-        for offset in REST:
-            kv_copy(j, offset).wait_recv()
+        arrive(kvbuf.at[j, pl.ds(0, len(REST))], kv_recv.at[j, 1])
         keys, values, valid = keys_of(REST)
         for g in range(heads):
             top_near, total_near, mixed_near = near[g]
@@ -396,8 +399,7 @@
         ssb[0] = jnp.broadcast_to(row, (8, rows))
         for i in range(1, n_tp):
             ss_copy(i).start()
-        for i in range(1, n_tp):
-            ss_copy(i).wait_recv()
+        arrive(ssb.at[pl.ds(1, n_tp - 1)], few_recv.at[0])
         row = jnp.sum(ssb[...], axis=0)[:1]
         column = jnp.transpose(jnp.broadcast_to(row, (rows, rows)))[:, :1]
         scale = lax.rsqrt(column * (1.0 / full_width) + 1e-5)
@@ -408,24 +410,19 @@
         ppb[0] = jnp.broadcast_to(pooled * closing[...] / n.astype(F32), (8, width))
         for i in range(1, n_ctx):
             pp_copy(i).start()
-        for i in range(1, n_ctx):
-            pp_copy(i).wait_recv()
+        arrive(ppb.at[pl.ds(1, n_ctx - 1)], few_recv.at[1])
         pooled = jnp.sum(ppb[...], axis=0)
         sqb[0] = jnp.broadcast_to(jnp.sum(pooled * pooled, axis=1, keepdims=True), (8, HEAD))
         for i in range(1, n_tp):
             sq_copy(i).start()
-        for i in range(1, n_tp):
-            sq_copy(i).wait_recv()
+        arrive(sqb.at[pl.ds(1, n_tp - 1)], few_recv.at[2])
         norms = jnp.sum(sqb[...], axis=0)[:, :1]
         res[e] = pooled * lax.rsqrt(norms * (1.0 / full_width) + 1e-6)
         for i in range(1, sections):
             fin_copy(i).start()
         arrive(res.at[1 - e], fin_recv.at[1 - e])
-        for i in range(1, n_ctx):
-            pp_copy(i).wait_send()
-        for i in range(1, n_tp):
-            sq_copy(i).wait_send()
-            ss_copy(i).wait_send()
+        for i, buf in enumerate((ssb, ppb, sqb)):
+            arrive(buf.at[pl.ds(1, buf.shape[0] - 1)], few_send.at[i])
         for i in range(1, sections):
             fin_copy(i).wait_send()
 
@@ -442,17 +439,11 @@
     for item in range(7):
         weight_copy(item).wait_send()
     for j in range(2):
-        for q in range(PIECES):
-            for d in range(2):
-                for r in range(3):
-                    ag_copy(j, d, r, q, agb.at[j, d, r]).wait_send()
-                for r in range(2):
-                    rs_copy(j, d, r, q).wait_send()
-                prt_copy(j, d, q).wait_send()
-            ag_far(j, q).wait_send()
-            rs_far(j, q).wait_send()
-        for offset in NEAR + REST:
-            kv_copy(j, offset).wait_send()
+        arrive(agb.at[j], ag_send.at[j, 0])
+        arrive(agf.at[j], ag_send.at[j, 1])
+        arrive(rso.at[j], rs_send.at[j, 0])
+        arrive(rsfo.at[j], rs_send.at[j, 1])
+        arrive(kvbuf.at[j, pl.ds(1, n_ctx - 1)], kv_send.at[j])
 
 
 def build(mesh):
@@ -523,21 +514,17 @@
                 dma((7,)),
                 dma((3,)),
                 dma((1,)),
+                dma((2, 2)),
                 dma((2, 2, 4, PIECES)),
-                dma((2, 2, 4, PIECES)),
-                dma((2, 2, 4, PIECES)),
+                dma((2, 2)),
                 dma((2, 2, 4, PIECES)),
                 dma((3, 2, PIECES)),
-                dma((2, n_ctx)),
-                dma((2, n_ctx)),
+                dma((2,)),
+                dma((2, 2)),
                 dma((2,)),
                 dma((2,)),
-                dma((n_tp,)),
-                dma((n_tp,)),
-                dma((n_ctx,)),
-                dma((n_ctx,)),
-                dma((n_tp,)),
-                dma((n_tp,)),
+                dma((3,)),
+                dma((3,)),
                 dma((sections,)),
                 dma((micro,)),
             ],

time: 182 us -> 178 us (0.978)
  Pallas kernels: 181 us -> 176 us
    pallas_call x1, Pallas kernels: 181 us -> 176 us  [shards(): pl.pallas_call(body, out_shape=jax.ShapeDtypeStruct((micro, width), F32),...]
where the time goes in v5:
time: 178 us
  Pallas kernels  176 us (99%)
    pallas_call x1, Pallas kernels, shards(): pl.pallas_call(body, out_shape=jax.ShapeDtypeStruct((micro, width), F32),...  176 us

profile of v5, /device:TPU:1, one launch (start us, length us, event | category | flops | bytes accessed | tf_op | source)
XLA Modules:
  0.0 177.6 jit_solution(16555932759246495887)
XLA Ops:
  0.0 176.3 %shard_map.136 = f32[2,512]{1,0:T(2,128)} custom-call(s32[2]{0:T(128)} %refs_0_.1, s32[2]{0:T(128)} %refs_1_.1, bf16[2,128,512]{2,1,0:T(8,128)(2,1)} %refs_2_.1, f32[1,4096]{1,0:T(1,128)} %refs_3_.1, f32[1,512]{1,0:T(1,128)} %bitcast.21, f32[8,2,128,128]{3,2,1,0:T(8,128)} %constant.2.clone.refs_5_, bf16[8,512,512]{2,1,0:T(8,128)(2,1)} %bitcast.13, ...), custom_call_target="tpu_custom_call" | custom-call | flops 3758096384 | bytes 16777216 | tf_op jit(solution)/shard_map/pallas_call | solution.py:477
  176.3 1.3 copy.16

commit v6 on v5

--- a/solution.py
+++ b/solution.py
@@ -56,6 +56,12 @@
     def around(at, by, n):
         return lax.rem(at + (by + n), n)
 
+    swap = n_ctx // 2
+    across = around(c, swap, n_ctx)
+
+    def place(at):
+        return jnp.where(first_pair, at, around(at, swap, n_ctx))
+
     def remote(src, dst, send, recv, section=s, ctx=c, tp=z):
         return pltpu.make_async_remote_copy(
             src_ref=src, dst_ref=dst, send_sem=send, recv_sem=recv, device_id=(section, ctx, tp),
@@ -94,7 +100,7 @@
     small_copies = [
         pltpu.make_async_copy(qd_hbm, qd, small_sem.at[0]),
         pltpu.make_async_copy(vd_hbm, vd, small_sem.at[1]),
-        pltpu.make_async_copy(tables.at[c], trig, small_sem.at[2]),
+        pltpu.make_async_copy(tables.at[place(c)], trig, small_sem.at[2]),
     ]
 
     @pl.when(first_pair)
@@ -111,7 +117,7 @@
     peers = [(s, c, around(z, i, n_tp)) for i in range(1, n_tp)]
     peers += [(s, around(c, i, n_ctx), z) for i in range(1, n_ctx)]
     peers += [(around(s, i, sections), c, z) for i in range(1, sections)]
-    peers += [(around(s, 2, sections), c, neighbour[d]) for d in range(2)]
+    peers += [(around(s, 2, sections), across, to) for to in (z,) + neighbour]
     for peer in peers:
         pl.semaphore_signal(barrier, 1, device_id=peer, device_id_type=MESH)
 
@@ -149,16 +155,17 @@
 
     def prt_copy(j, d, q):
         slot = jnp.where(j == 0, 1, jnp.where(last_pair, 2, 0))
-        where = jnp.where((j == 1) & jnp.logical_not(last_pair), around(s, 2, sections), s)
+        moves = (j == 1) & jnp.logical_not(last_pair)
         return remote(rso.at[j, d, 2, span(q)], prt.at[slot, d, span(q)], rs_send.at[j, 0],
-                      prt_recv.at[slot, d, q], tp=neighbour[d], section=where)
+                      prt_recv.at[slot, d, q], tp=neighbour[d], ctx=jnp.where(moves, across, c),
+                      section=jnp.where(moves, around(s, 2, sections), s))
 
     def pass_copy(buf, i):
-        return remote(buf.at[2], buf.at[0], pass_send.at[i], pass_recv.at[i], section=around(s, 2, sections))
+        return remote(buf.at[2], buf.at[0], pass_send.at[i], pass_recv.at[i], ctx=across,
+                      section=around(s, 2, sections))
 
     def ctx_peer(dy, dx):
-        across = n_ctx // 2
-        return around(c // across, dy, 2) * across + around(lax.rem(c, across), dx, across)
+        return around(c // swap, dy, 2) * swap + around(lax.rem(c, swap), dx, swap)
 
     ctx_ids = {offset: ctx_peer(*offset) for offset in NEAR + REST}
 
@@ -308,7 +315,7 @@
         def keys_of(offsets):
             sources = [ctx_peer(-dy, -dx) for dy, dx in offsets]
             blocks = [kvbuf[j, source] for source in sources]
-            valid = jnp.concatenate([lane + source * rows < n for source in sources], axis=1)
+            valid = jnp.concatenate([lane + place(source) * rows < n for source in sources], axis=1)
             return (jnp.concatenate([block[:, :HEAD] for block in blocks], axis=0),
                     jnp.concatenate([block[:, HEAD:] for block in blocks], axis=0), valid)
 
@@ -404,7 +411,7 @@
         column = jnp.transpose(jnp.broadcast_to(row, (rows, rows)))[:, :1]
         scale = lax.rsqrt(column * (1.0 / full_width) + 1e-5)
         n = lengths[e]
-        position = c * rows + lax.broadcasted_iota(jnp.int32, (rows, 1), 0)
+        position = place(c) * rows + lax.broadcasted_iota(jnp.int32, (rows, 1), 0)
         scale = jnp.where(position < n, scale, 0.0)
         pooled = jnp.sum(hidden[3].astype(F32) * scale, axis=0, keepdims=True)
         ppb[0] = jnp.broadcast_to(pooled * closing[...] / n.astype(F32), (8, width))

time: 178 us -> 177 us (level)
  no operation moved by 1% of the time
where the time goes in v6:
time: 177 us
  Pallas kernels  176 us (99%)
    pallas_call x1, Pallas kernels, shards(): pl.pallas_call(body, out_shape=jax.ShapeDtypeStruct((micro, width), F32),...  176 us

profile of v6, /device:TPU:1, one launch (start us, length us, event | category | flops | bytes accessed | tf_op | source)
XLA Modules:
  0.0 177.2 jit_solution(16023918293832117597)
XLA Ops:
  0.0 175.9 %shard_map.136 = f32[2,512]{1,0:T(2,128)} custom-call(s32[2]{0:T(128)} %refs_0_.1, s32[2]{0:T(128)} %refs_1_.1, bf16[2,128,512]{2,1,0:T(8,128)(2,1)} %refs_2_.1, f32[1,4096]{1,0:T(1,128)} %refs_3_.1, f32[1,512]{1,0:T(1,128)} %bitcast.21, f32[8,2,128,128]{3,2,1,0:T(8,128)} %constant.2.clone.refs_5_, bf16[8,512,512]{2,1,0:T(8,128)(2,1)} %bitcast.13, ...), custom_call_target="tpu_custom_call" | custom-call | flops 3758096384 | bytes 16777216 | tf_op jit(solution)/shard_map/pallas_call | solution.py:484
  175.9 1.3 copy.16

commit v7 on v6

--- a/solution.py
+++ b/solution.py
@@ -121,15 +121,16 @@
     for peer in peers:
         pl.semaphore_signal(barrier, 1, device_id=peer, device_id_type=MESH)
 
-    for copy in small_copies:
-        copy.wait()
-    for slot, document in ((e, e), (2, 1 - e)):
-        t = tenants[document]
-        up[slot] = jnp.zeros(up.shape[1:], BF16)
-        down[slot, :rank] = qd[t]
-        down[slot, rank:] = vd[t]
-        up[slot, :rank, :heads * HEAD] = q_up[t]
-        up[slot, rank:, heads * HEAD:] = v_up[t]
+    def pick_adapters():
+        for copy in small_copies:
+            copy.wait()
+        for slot, document in ((e, e), (2, 1 - e)):
+            t = tenants[document]
+            up[slot] = jnp.zeros(up.shape[1:], BF16)
+            down[slot, :rank] = qd[t]
+            down[slot, rank:] = vd[t]
+            up[slot, :rank, :heads * HEAD] = q_up[t]
+            up[slot, rank:, heads * HEAD:] = v_up[t]
 
     pl.semaphore_wait(barrier, len(peers))
 
@@ -236,7 +237,10 @@
 
         @pl.when(first_pair & (j == 0))
         def _():
-            for item in (GAIN, DOWN, UP, WK, WV, WQ):
+            for item in (WK, WV, WQ, GAIN):
+                weight_copy(item).start()
+            pick_adapters()
+            for item in (DOWN, UP):
                 weight_copy(item).start()
 
         @pl.when((j == 1) & jnp.logical_not(last_pair))
@@ -391,7 +395,10 @@
 
     @pl.when(jnp.logical_not(first_pair))
     def _():
-        for item in (GAIN, DOWN, UP, WK, WV, WQ, WO):
+        for item in (WK, WV, WQ, WO, GAIN):
+            weight_copy(item).start()
+        pick_adapters()
+        for item in (DOWN, UP):
             weight_copy(item).start()
 
     lax.fori_loop(0, 2, layer, 0)

time: 177 us -> 178 us (level)
  no operation moved by 1% of the time
where the time goes in v7:
time: 178 us; the launch traced here: 177 us
  Pallas kernels  176 us (99%)
    pallas_call x1, Pallas kernels, shards(): pl.pallas_call(body, out_shape=jax.ShapeDtypeStruct((micro, width), F32),...  176 us

profile of v7, /device:TPU:1, one launch (start us, length us, event | category | flops | bytes accessed | tf_op | source)
XLA Modules:
  0.0 177.5 jit_solution(9559511916841562926)
XLA Ops:
  0.0 176.2 %shard_map.136 = f32[2,512]{1,0:T(2,128)} custom-call(s32[2]{0:T(128)} %refs_0_.1, s32[2]{0:T(128)} %refs_1_.1, bf16[2,128,512]{2,1,0:T(8,128)(2,1)} %refs_2_.1, f32[1,4096]{1,0:T(1,128)} %refs_3_.1, f32[1,512]{1,0:T(1,128)} %bitcast.21, f32[8,2,128,128]{3,2,1,0:T(8,128)} %constant.2.clone.refs_5_, bf16[8,512,512]{2,1,0:T(8,128)(2,1)} %bitcast.13, ...), custom_call_target="tpu_custom_call" | custom-call | flops 3758096384 | bytes 16777216 | tf_op jit(solution)/shard_map/pallas_call | solution.py:491
  176.2 1.3 copy.16

commit v8 on v7

--- a/solution.py
+++ b/solution.py
@@ -13,7 +13,7 @@
 BF16 = jnp.bfloat16
 MESH = pl.DeviceIdType.MESH
 
-PIECES = 4
+PIECES = 8
 FAR = 3
 WK, WV, WQ, GAIN, WO, DOWN, UP = range(7)
 NEAR = ((1, 0), (0, 1), (0, 3))

time: 178 us -> 176 us (0.989)
  no operation moved by 1% of the time
where the time goes in v8:
time: 176 us
  Pallas kernels  175 us (99%)
    pallas_call x1, Pallas kernels, shards(): pl.pallas_call(body, out_shape=jax.ShapeDtypeStruct((micro, width), F32),...  175 us

profile of v8, /device:TPU:1, one launch (start us, length us, event | category | flops | bytes accessed | tf_op | source)
XLA Modules:
  0.0 176.0 jit_solution(9400011011610437425)
XLA Ops:
  0.0 174.7 %shard_map.136 = f32[2,512]{1,0:T(2,128)} custom-call(s32[2]{0:T(128)} %refs_0_.1, s32[2]{0:T(128)} %refs_1_.1, bf16[2,128,512]{2,1,0:T(8,128)(2,1)} %refs_2_.1, f32[1,4096]{1,0:T(1,128)} %refs_3_.1, f32[1,512]{1,0:T(1,128)} %bitcast.21, f32[8,2,128,128]{3,2,1,0:T(8,128)} %constant.2.clone.refs_5_, bf16[8,512,512]{2,1,0:T(8,128)(2,1)} %bitcast.13, ...), custom_call_target="tpu_custom_call" | custom-call | flops 3758096384 | bytes 16777216 | tf_op jit(solution)/shard_map/pallas_call | solution.py:491
  174.7 1.3 copy.16

commit v9 on v8

--- a/solution.py
+++ b/solution.py
@@ -18,6 +18,7 @@
 WK, WV, WQ, GAIN, WO, DOWN, UP = range(7)
 NEAR = ((1, 0), (0, 1), (0, 3))
 REST = ((1, 1), (1, 3), (0, 2), (1, 2))
+FIRST = REST[2:]
 
 
 def fold(x):
@@ -304,7 +305,7 @@
         kvbuf[j, c, :, :HEAD] = rotate(kv[:, :HEAD]).astype(BF16)
         added = jnp.dot(low, up[j, :, heads * HEAD:], preferred_element_type=F32)
         kvbuf[j, c, :, HEAD:] = (kv[:, HEAD:] + added).astype(BF16)
-        for offset in NEAR + REST:
+        for offset in FIRST + NEAR + REST[:2]:
             kv_copy(j, offset).start()
         take(j, pair(2) + far, others=False)
         factor = HEAD ** -0.5 * math.log2(math.e)

time: 176 us -> 174 us (0.989)
  Pallas kernels: 175 us -> 173 us
    pallas_call x1, Pallas kernels: 175 us -> 173 us  [shards(): pl.pallas_call(body, out_shape=jax.ShapeDtypeStruct((micro, width), F32),...]
where the time goes in v9:
time: 174 us
  Pallas kernels  173 us (99%)
    pallas_call x1, Pallas kernels, shards(): pl.pallas_call(body, out_shape=jax.ShapeDtypeStruct((micro, width), F32),...  173 us

profile of v9, /device:TPU:1, one launch (start us, length us, event | category | flops | bytes accessed | tf_op | source)
XLA Modules:
  0.0 173.9 jit_solution(17206462298082276602)
XLA Ops:
  0.0 172.6 %shard_map.136 = f32[2,512]{1,0:T(2,128)} custom-call(s32[2]{0:T(128)} %refs_0_.1, s32[2]{0:T(128)} %refs_1_.1, bf16[2,128,512]{2,1,0:T(8,128)(2,1)} %refs_2_.1, f32[1,4096]{1,0:T(1,128)} %refs_3_.1, f32[1,512]{1,0:T(1,128)} %bitcast.21, f32[8,2,128,128]{3,2,1,0:T(8,128)} %constant.2.clone.refs_5_, bf16[8,512,512]{2,1,0:T(8,128)(2,1)} %bitcast.13, ...), custom_call_target="tpu_custom_call" | custom-call | flops 3758096384 | bytes 16777216 | tf_op jit(solution)/shard_map/pallas_call | solution.py:492
  172.7 1.3 copy.16
